TPU v7x, 256 devices: a whole 4x4x8 slice. The times are simulated.
256 devices in a mesh: tm: 128 (over y, z, x_lo, core), band: 2 (over x_hi).
Axes of the slice: x: 4 (x_hi: 2, x_lo: 2; x = x_hi * 2 + x_lo), y: 4, z: 8, core: 2. Of those that a mesh axis runs over, the one named last changes fastest.
Arguments:
- phonon: float32 [256, 256, 256], P('tm', 'band'), may hold values from -4 to 4
- momentum: float32 [256, 256, 256], P('tm', 'band'), may hold values from -6 to 6
- source: float32 [256, 256, 256], P('tm', 'band'), may hold values from -6 to 6
- guess: float32 [256, 256, 256], P('tm', 'band'), may hold values from -4 to 4
- bonds: int32 [2, 256, 256], P(None, 'band'), may hold values 0 or 1
Outputs:
- solution: float32 [256, 256, 256], P('tm', 'band')
- momentum_new: float32 [256, 256, 256], P('tm', 'band')
All inputs are finite; a program needn't handle non-finite values. No bound on the sum of `bonds` on one device may be relied on, other than what follows from the above.
Results may differ from a plain program's by a relative error of at most 0.000064.
Values sent between devices are 32-bit elements; how exact they have to be, the bound alone decides.
A program may use at most 64 MiB of HBM per device.

v0:
```python
import math

import jax
import jax.numpy as jnp
from jax import lax
from jax.sharding import PartitionSpec as P

ORDER = 24


hop_angle = 0.3
coupling = 0.2
stiffness = 1.0
mass_term = 0.5
relaxation = 0.25
step_size = 0.25
cheb_base = 4.03
cheb_slope = 0.5
half_width = 4.0


def extended(value, sides, width):
    for axis, dim in sides:
        size, length = (lax.axis_size(axis), value.shape[dim])
        up = [(i, (i + 1) % size) for i in range(size)]
        down = [(j, i) for i, j in up]
        last = lax.slice_in_dim(value, length - width, length, axis=dim)
        leading = lax.slice_in_dim(value, 0, width, axis=dim)
        before = lax.ppermute(last, axis, up)
        after = lax.ppermute(leading, axis, down)
        value = jnp.concatenate([before, value, after], axis=dim)
    return value


def passed_along(value, axis, by):
    size = lax.axis_size(axis)
    return lax.ppermute(value, axis, [(i, (i + by) % size) for i in range(size)])


def dft_basis(length_total):
    rows = lax.broadcasted_iota(jnp.int32, (length_total, length_total), 0)
    columns = lax.broadcasted_iota(jnp.int32, (length_total, length_total), 1)
    phase = (2 * (rows // 2) + 1) * columns % (2 * length_total)
    angle = phase.astype(jnp.float32) * (math.pi / length_total)
    return math.sqrt(2.0 / length_total) * jnp.where(rows % 2 == 0, jnp.cos(angle), jnp.sin(angle))


def cheb_centre(index, length_total):
    angle = (2 * (index // 2) + 1).astype(jnp.float32) * (math.pi / length_total)
    return cheb_base + cheb_slope * (1.0 - jnp.cos(angle))


def pair_tables(horizontal, vertical, vertical_prev, row_even, column_even):
    horizontal_prev = jnp.roll(horizontal, 1, 1)
    vertical_up = jnp.roll(vertical, 1, 0)
    strengths = (
        jnp.where(column_even, horizontal, horizontal_prev),
        jnp.where(column_even, horizontal_prev, horizontal),
        jnp.where(row_even, vertical, vertical_up),
        jnp.where(row_even, vertical_prev, vertical),
    )
    return tuple(
        ((jnp.cosh(hop_angle * strength), jnp.sinh(hop_angle * strength)) for strength in strengths)
    )


def partner_of(vector, colour, row_even, column_even):
    if colour == 0:
        return jnp.where(column_even, jnp.roll(vector, -1, 2), jnp.roll(vector, 1, 2))
    if colour == 1:
        return jnp.where(column_even, jnp.roll(vector, 1, 2), jnp.roll(vector, -1, 2))
    if colour == 2:
        return jnp.where(row_even, jnp.roll(vector, -1, 1), jnp.roll(vector, 1, 1))
    padded = extended(vector, (("band", 1),), 1)
    return jnp.where(row_even, padded[:, :-2], padded[:, 2:])


def to_spectrum(piece):
    basis = dft_basis(piece.shape[0])
    return jnp.einsum("kl,lrc->krc", basis, piece, precision=lax.Precision.HIGHEST)


def to_slices(piece):
    basis = dft_basis(piece.shape[0])
    return jnp.einsum("kl,krc->lrc", basis, piece, precision=lax.Precision.HIGHEST)


def shards(phonon, momentum, source, guess, bonds):
    slice_count, row_count, col_count = guess.shape
    cycle_size = lax.axis_size("tm")
    position = lax.axis_index("tm")
    grid_shape = (row_count, col_count)
    row_even = lax.broadcasted_iota(jnp.int32, grid_shape, 0) % 2 == 0
    column_even = lax.broadcasted_iota(jnp.int32, grid_shape, 1) % 2 == 0
    edge_bonds = passed_along(bonds[1][-1:], "band", 1)
    vertical_prev = jnp.concatenate([edge_bonds, bonds[1][:-1]], 0)
    tables = pair_tables(
        bonds[0].astype(jnp.float32),
        bonds[1].astype(jnp.float32),
        vertical_prev.astype(jnp.float32),
        row_even,
        column_even,
    )

    def apply_pairs(vector, colours):
        for colour in colours:
            cosh_part, sinh_part = tables[colour]
            vector = cosh_part * vector + sinh_part * partner_of(
                vector, colour, row_even, column_even
            )
        return vector

    phonon_rims = extended(phonon, (("tm", 0),), 1)
    factor_wide = jnp.exp(-coupling * phonon_rims)
    expo = factor_wide[1:-1]
    first_sign = jnp.where(position == 0, -1.0, 1.0).astype(jnp.float32)
    last_sign = jnp.where(position == cycle_size - 1, -1.0, 1.0).astype(jnp.float32)

    def from_prev(piece):
        return passed_along(piece, "tm", 1) * first_sign

    def from_after(piece):
        return passed_along(piece, "tm", -1) * last_sign

    applied = apply_pairs(expo * guess, (0, 1, 2, 3))
    link = guess - jnp.concatenate([from_prev(applied[-1:]), applied[:-1]], 0)
    shifted = jnp.concatenate([link[1:], from_after(link[:1])], 0)
    normal = link - expo * apply_pairs(shifted, (3, 2, 1, 0))
    residual = source - normal
    mixed = to_spectrum(lax.all_to_all(residual, "tm", split_axis=1, concat_axis=0, tiled=True))
    spectrum = lax.all_to_all(mixed, "tm", split_axis=0, concat_axis=1, tiled=True)
    freq_index = position * slice_count + jnp.arange(slice_count, dtype=jnp.int32)
    centre = cheb_centre(freq_index, slice_count * cycle_size)[:, None, None]
    ratio = centre / half_width
    start = (jnp.zeros_like(spectrum), spectrum, spectrum / centre, 1.0 / ratio)

    def sweep_each(counter, carry):
        accum, remaining, direction, weight_now = carry
        padded = extended(direction, (("band", 1),), 1)
        beside_all = (
            padded[:, :-2] + padded[:, 2:] + jnp.roll(direction, 1, 2) + jnp.roll(direction, -1, 2)
        )
        accum = accum + direction
        remaining = remaining - (centre * direction - beside_all)
        weight_new = 1.0 / (2.0 * ratio - weight_now)
        direction = weight_new * weight_now * direction + 2.0 * weight_new / half_width * remaining
        return (accum, remaining, direction, weight_new)

    accum = lax.fori_loop(0, ORDER, sweep_each, start)[0]
    mixed_back = to_slices(lax.all_to_all(accum, "tm", split_axis=1, concat_axis=0, tiled=True))
    timed = lax.all_to_all(mixed_back, "tm", split_axis=0, concat_axis=1, tiled=True)
    solution = guess + relaxation * timed
    propagated = apply_pairs(expo * solution, (0, 1, 2, 3))
    image = solution - jnp.concatenate([from_prev(propagated[-1:]), propagated[:-1]], 0)
    pulled = apply_pairs(jnp.concatenate([image[1:], from_after(image[:1])], 0), (3, 2, 1, 0))
    fermion_force = -2.0 * coupling * expo * solution * pulled
    boson_force = (
        stiffness * (2.0 * phonon - phonon_rims[:-2] - phonon_rims[2:]) + mass_term * phonon
    )
    momentum_new = momentum - step_size * (boson_force + fermion_force)
    return (solution, momentum_new)


def solution(mesh):
    return jax.shard_map(
        shards,
        mesh=mesh,
        in_specs=(
            P("tm", "band", None),
            P("tm", "band", None),
            P("tm", "band", None),
            P("tm", "band", None),
            P(None, "band", None),
        ),
        out_specs=(P("tm", "band", None), P("tm", "band", None)),
        check_vma=False,
    )
```

profile of v0, /device:TPU:1, one launch (start us, length us, event | category | flops | bytes accessed | tf_op | source)
XLA Modules:
  0.0 338.2 jit_solution(2155616920549901178)
XLA Ops:
  1.3 3.6 %collective-permute-start.2 = (s32[1,256]{1,0:T(1,128)S(1)}, s32[1,256]{1,0:T(1,128)S(1)}, u32[]{:S(2)}, u32[]{:S(2)}) collective-permute-start(s32[1,256]{1,0:T(1,128)S(1)} %slice_bitcast_fusion.2), channel_id=1, source_target_pairs={{0,1},{1,0},{2,3},{3,2},{4,5},{5,4},{6,7},{7,6},{8,9},{9,8},{10,11... | collective-permute-start | bytes 3080 | tf_op jit(solution)/shard_map/ppermute | solution.py:37
  9.1 2.4 collective-permute-done.4
  19.4 7.0 %collective-permute-done.7 = f32[1,128,256]{2,1,0:T(8,128)S(1)} collective-permute-done((f32[1,128,256]{2,1,0:T(8,128)S(1)}, f32[1,128,256]{2,1,0:T(8,128)S(1)}, u32[]{:S(2)}, u32[]{:S(2)}) %collective-permute-start.7) | collective-permute-done | bytes 131104 | tf_op jit(solution)/shard_map/ppermute | solution.py:37
  26.5 7.9 %collective-permute-start.8 = (f32[1,128,256]{2,1,0:T(8,128)S(1)}, f32[1,128,256]{2,1,0:T(8,128)S(1)}, u32[]{:S(2)}, u32[]{:S(2)}) collective-permute-start(f32[1,128,256]{2,1,0:T(8,128)S(1)} %get-tuple-element.249), channel_id=1, source_target_pairs={{0,254},{2,0},{4,2},{6,4},{8,6},{10,8},{12,10},{14,12},{16,14},{18... | collective-permute-start | bytes 393224 | tf_op jit(solution)/shard_map/ppermute | solution.py:37
  43.5 9.9 %all-to-all-start = ((f32[2,128,256]{2,0,1:T(2,128)}), f32[2,128,256]{2,0,1:T(2,128)S(1)}, u32[]{:S(2)}, u32[]{:S(2)}) async-start(f32[2,128,256]{2,0,1:T(2,128)} %copy.234), calls=%async_computation | async-start | bytes 524288 | tf_op jit(solution)/shard_map/all_to_all | solution.py:130
  53.4 14.3 %all-to-all-done = f32[2,128,256]{2,0,1:T(2,128)S(1)} async-done(((f32[2,128,256]{2,0,1:T(2,128)}), f32[2,128,256]{2,0,1:T(2,128)S(1)}, u32[]{:S(2)}, u32[]{:S(2)}) %all-to-all-start) | async-done | bytes 262176 | tf_op jit(solution)/shard_map/all_to_all | solution.py:130
  67.8 2.5 convolution_bitcast_fusion.1
  71.3 5.7 %all-to-all-start.1 = ((f32[256,1,256]{2,1,0:T(1,128)}), f32[256,1,256]{2,1,0:T(1,128)S(1)}, u32[]{:S(2)}, u32[]{:S(2)}) async-start(f32[256,1,256]{2,1,0:T(1,128)} %copy.235), calls=%async_computation.1 | async-start | bytes 524288 | tf_op jit(solution)/shard_map/all_to_all | solution.py:131
  77.1 14.3 %all-to-all-done.1 = f32[256,1,256]{2,1,0:T(1,128)S(1)} async-done(((f32[256,1,256]{2,1,0:T(1,128)}), f32[256,1,256]{2,1,0:T(1,128)S(1)}, u32[]{:S(2)}, u32[]{:S(2)}) %all-to-all-start.1) | async-done | bytes 262176 | tf_op jit(solution)/shard_map/all_to_all | solution.py:131
  91.5 143.8 %while.21 = (s32[]{:T(128)}, f32[2,128,256]{2,1,0:T(8,128)S(1)}, f32[2,128,256]{2,1,0:T(8,128)S(1)}, f32[2,128,256]{2,1,0:T(8,128)S(1)}, f32[2,1,1]{0,2,1:T(1,12...) while((s32[]{:T(128)}, f32[2,128,256]{2,1,0:T(8,128)S(1)}, ...), condition=%wide.region_1.2_spmd.clone.clone.clone, body=%wide.region_0.1_spmd.clone.clone.clone.sunk | while | flops 983146 | bytes 3698975 | solution.py:149
  91.6 2.8 collective-permute-start
  95.6 2.7 collective-permute-done.1
  99.1 2.7 collective-permute-start.1
  103.5 2.8 collective-permute-start
  107.6 2.7 collective-permute-done.1
  111.1 2.7 collective-permute-start.1
  115.5 2.8 collective-permute-start
  119.5 2.7 collective-permute-done.1
  123.0 2.7 collective-permute-start.1
  127.4 2.8 collective-permute-start
  131.5 2.7 collective-permute-done.1
  135.0 2.7 collective-permute-start.1
  139.4 2.8 collective-permute-start
  143.4 2.7 collective-permute-done.1
  146.9 2.7 collective-permute-start.1
  151.3 2.8 collective-permute-start
  155.4 2.7 collective-permute-done.1
  159.2 2.4 collective-permute-start.1
  163.6 2.5 collective-permute-start
  175.6 2.5 collective-permute-start
  187.6 2.4 collective-permute-start
  191.6 2.6 collective-permute-done.1
  195.1 2.6 collective-permute-start.1
  199.5 2.7 collective-permute-start
  203.6 2.6 collective-permute-done.1
  207.1 2.6 collective-permute-start.1
  211.5 2.7 collective-permute-start
  215.5 2.7 collective-permute-done.1
  219.0 2.7 collective-permute-start.1
  223.5 2.7 collective-permute-start
  227.5 2.6 collective-permute-done.1
  231.0 2.6 collective-permute-start.1
  235.6 53.4 %all_to_all.57 = f32[2,128,256]{2,0,1:T(2,128)S(1)} all-to-all(f32[2,128,256]{2,0,1:T(2,128)S(1)} %copy.237), channel_id=1, replica_groups=mesh['tm'=128,'band'=2] {'tm'}, dimensions={1} | all-to-all | bytes 524288 | tf_op jit(solution)/shard_map/all_to_all | solution.py:150
  291.1 19.5 %all_to_all.58 = f32[256,1,256]{2,1,0:T(1,128)S(1)} all-to-all(f32[256,1,256]{2,1,0:T(1,128)S(1)} %copy.238), channel_id=1, replica_groups=mesh['tm'=128,'band'=2] {'tm'}, dimensions={0} | all-to-all | bytes 524288 | tf_op jit(solution)/shard_map/all_to_all | solution.py:151
  312.6 2.8 collective-permute-start.11
  316.7 2.7 collective-permute-done.12
  323.6 6.6 %collective-permute-start.14 = (f32[1,128,256]{2,1,0:T(8,128)S(1)}, f32[1,128,256]{2,1,0:T(8,128)S(1)}, u32[]{:S(2)}, u32[]{:S(2)}) collective-permute-start(f32[1,128,256]{2,1,0:T(8,128)S(1)} %get-tuple-element.217), channel_id=1, source_target_pairs={{0,254},{2,0},{4,2},{6,4},{8,6},{10,8},{12,10},{14,12},{16,14},{18... | collective-permute-start | bytes 393224 | tf_op jit(solution)/shard_map/ppermute | solution.py:37
  331.5 2.8 collective-permute-start.16
  (360 shorter events, 94.6 us)
Async XLA Ops:
  1.3 6.5 %collective-permute-start.2 = (s32[1,256]{1,0:T(1,128)S(1)}, s32[1,256]{1,0:T(1,128)S(1)}, u32[]{:S(2)}, u32[]{:S(2)}) collective-permute-start(s32[1,256]{1,0:T(1,128)S(1)} %slice_bitcast_fusion.2), channel_id=1, source_target_pairs={{0,1},{1,0},{2,3},{3,2},{4,5},{5,4},{6,7},{7,6},{8,9},{9,8},{10,11... | collective-permute-start | bytes 3080 | tf_op jit(solution)/shard_map/ppermute | solution.py:37
  7.1 4.4 %collective-permute-start.4 = (f32[1,128,256]{2,1,0:T(8,128)S(1)}, f32[1,128,256]{2,1,0:T(8,128)S(1)}, u32[]{:S(2)}, u32[]{:S(2)}) collective-permute-start(f32[1,128,256]{2,1,0:T(8,128)S(1)} %get-tuple-element.269), channel_id=1, source_target_pairs={{2,0},{4,2},{6,4},{8,6},{10,8},{12,10},{14,12},{16,14},{18,16},{20... | collective-permute-start | bytes 393224 | tf_op jit(solution)/shard_map/ppermute | solution.py:30
  12.6 4.1 %collective-permute-start.5 = (f32[2,1,256]{2,1,0:T(1,128)S(1)}, f32[2,1,256]{2,1,0:T(1,128)S(1)}, u32[]{:S(2)}, u32[]{:S(2)}) collective-permute-start(f32[2,1,256]{2,1,0:T(1,128)S(1)} %get-tuple-element.252), channel_id=1, source_target_pairs={{0,1},{1,0},{2,3},{3,2},{4,5},{5,4},{6,7},{7,6},{8,9},{9,8},{10,11... | collective-permute-start | bytes 6152 | tf_op jit(solution)/shard_map/ppermute | solution.py:29
  14.4 3.9 %collective-permute-start.6 = (f32[2,1,256]{2,1,0:T(1,128)S(1)}, f32[2,1,256]{2,1,0:T(1,128)S(1)}, u32[]{:S(2)}, u32[]{:S(2)}) collective-permute-start(f32[2,1,256]{2,1,0:T(1,128)S(1)} %get-tuple-element.253), channel_id=1, source_target_pairs={{1,0},{0,1},{3,2},{2,3},{5,4},{4,5},{7,6},{6,7},{9,8},{8,9},{11,10... | collective-permute-start | bytes 6152 | tf_op jit(solution)/shard_map/ppermute | solution.py:30
  18.4 7.9 %collective-permute-start.7 = (f32[1,128,256]{2,1,0:T(8,128)S(1)}, f32[1,128,256]{2,1,0:T(8,128)S(1)}, u32[]{:S(2)}, u32[]{:S(2)}) collective-permute-start(f32[1,128,256]{2,1,0:T(8,128)S(1)} %get-tuple-element.250), channel_id=1, source_target_pairs={{0,2},{2,4},{4,6},{6,8},{8,10},{10,12},{12,14},{14,16},{16,18},{18... | collective-permute-start | bytes 393224 | tf_op jit(solution)/shard_map/ppermute | solution.py:37
  26.5 8.8 %collective-permute-start.8 = (f32[1,128,256]{2,1,0:T(8,128)S(1)}, f32[1,128,256]{2,1,0:T(8,128)S(1)}, u32[]{:S(2)}, u32[]{:S(2)}) collective-permute-start(f32[1,128,256]{2,1,0:T(8,128)S(1)} %get-tuple-element.249), channel_id=1, source_target_pairs={{0,254},{2,0},{4,2},{6,4},{8,6},{10,8},{12,10},{14,12},{16,14},{18... | collective-permute-start | bytes 393224 | tf_op jit(solution)/shard_map/ppermute | solution.py:37
  35.3 4.0 %collective-permute-start.9 = (f32[2,1,256]{2,1,0:T(1,128)S(1)}, f32[2,1,256]{2,1,0:T(1,128)S(1)}, u32[]{:S(2)}, u32[]{:S(2)}) collective-permute-start(f32[2,1,256]{2,1,0:T(1,128)S(1)} %get-tuple-element.246), channel_id=1, source_target_pairs={{0,1},{1,0},{2,3},{3,2},{4,5},{5,4},{6,7},{7,6},{8,9},{9,8},{10,11... | collective-permute-start | bytes 6152 | tf_op jit(solution)/shard_map/ppermute | solution.py:29
  36.7 3.9 %collective-permute-start.10 = (f32[2,1,256]{2,1,0:T(1,128)S(1)}, f32[2,1,256]{2,1,0:T(1,128)S(1)}, u32[]{:S(2)}, u32[]{:S(2)}) collective-permute-start(f32[2,1,256]{2,1,0:T(1,128)S(1)} %get-tuple-element.247), channel_id=1, source_target_pairs={{1,0},{0,1},{3,2},{2,3},{5,4},{4,5},{7,6},{6,7},{9,8},{8,9},{11,10... | collective-permute-start | bytes 6152 | tf_op jit(solution)/shard_map/ppermute | solution.py:30
  43.5 24.1 %all-to-all-start = ((f32[2,128,256]{2,0,1:T(2,128)}), f32[2,128,256]{2,0,1:T(2,128)S(1)}, u32[]{:S(2)}, u32[]{:S(2)}) async-start(f32[2,128,256]{2,0,1:T(2,128)} %copy.234), calls=%async_computation | async-start | bytes 524288 | tf_op jit(solution)/shard_map/all_to_all | solution.py:130
  71.3 20.1 %all-to-all-start.1 = ((f32[256,1,256]{2,1,0:T(1,128)}), f32[256,1,256]{2,1,0:T(1,128)S(1)}, u32[]{:S(2)}, u32[]{:S(2)}) async-start(f32[256,1,256]{2,1,0:T(1,128)} %copy.235), calls=%async_computation.1 | async-start | bytes 524288 | tf_op jit(solution)/shard_map/all_to_all | solution.py:131
  91.6 4.0 %collective-permute-start = (f32[2,1,256]{2,1,0:T(1,128)S(1)}, f32[2,1,256]{2,1,0:T(1,128)S(1)}, u32[]{:S(2)}, u32[]{:S(2)}) collective-permute-start(f32[2,1,256]{2,1,0:T(1,128)S(1)} %get-tuple-element.333), channel_id=1, source_target_pairs={{1,0},{0,1},{3,2},{2,3},{5,4},{4,5},{7,6},{6,7},{9,8},{8,9},{11,10... | collective-permute-start | bytes 6152 | tf_op jit(solution)/shard_map/while/body/eval_jaxpr/ppermute | solution.py:30
  94.4 3.9 %collective-permute-start.1 = (f32[2,1,256]{2,1,0:T(1,128)S(1)}, f32[2,1,256]{2,1,0:T(1,128)S(1)}, u32[]{:S(2)}, u32[]{:S(2)}) collective-permute-start(f32[2,1,256]{2,1,0:T(1,128)S(1)} %get-tuple-element.334), channel_id=1, source_target_pairs={{0,1},{1,0},{2,3},{3,2},{4,5},{5,4},{6,7},{7,6},{8,9},{9,8},{10,11... | collective-permute-start | bytes 6152 | tf_op jit(solution)/shard_map/while/body/eval_jaxpr/ppermute | solution.py:29
  98.8 4.0 %collective-permute-start = (f32[2,1,256]{2,1,0:T(1,128)S(1)}, f32[2,1,256]{2,1,0:T(1,128)S(1)}, u32[]{:S(2)}, u32[]{:S(2)}) collective-permute-start(f32[2,1,256]{2,1,0:T(1,128)S(1)} %get-tuple-element.333), channel_id=1, source_target_pairs={{1,0},{0,1},{3,2},{2,3},{5,4},{4,5},{7,6},{6,7},{9,8},{8,9},{11,10... | collective-permute-start | bytes 6152 | tf_op jit(solution)/shard_map/while/body/eval_jaxpr/ppermute | solution.py:30
  99.1 3.9 %collective-permute-start.1 = (f32[2,1,256]{2,1,0:T(1,128)S(1)}, f32[2,1,256]{2,1,0:T(1,128)S(1)}, u32[]{:S(2)}, u32[]{:S(2)}) collective-permute-start(f32[2,1,256]{2,1,0:T(1,128)S(1)} %get-tuple-element.334), channel_id=1, source_target_pairs={{0,1},{1,0},{2,3},{3,2},{4,5},{5,4},{6,7},{7,6},{8,9},{9,8},{10,11... | collective-permute-start | bytes 6152 | tf_op jit(solution)/shard_map/while/body/eval_jaxpr/ppermute | solution.py:29
  103.5 4.0 %collective-permute-start = (f32[2,1,256]{2,1,0:T(1,128)S(1)}, f32[2,1,256]{2,1,0:T(1,128)S(1)}, u32[]{:S(2)}, u32[]{:S(2)}) collective-permute-start(f32[2,1,256]{2,1,0:T(1,128)S(1)} %get-tuple-element.333), channel_id=1, source_target_pairs={{1,0},{0,1},{3,2},{2,3},{5,4},{4,5},{7,6},{6,7},{9,8},{8,9},{11,10... | collective-permute-start | bytes 6152 | tf_op jit(solution)/shard_map/while/body/eval_jaxpr/ppermute | solution.py:30
  106.3 3.9 %collective-permute-start.1 = (f32[2,1,256]{2,1,0:T(1,128)S(1)}, f32[2,1,256]{2,1,0:T(1,128)S(1)}, u32[]{:S(2)}, u32[]{:S(2)}) collective-permute-start(f32[2,1,256]{2,1,0:T(1,128)S(1)} %get-tuple-element.334), channel_id=1, source_target_pairs={{0,1},{1,0},{2,3},{3,2},{4,5},{5,4},{6,7},{7,6},{8,9},{9,8},{10,11... | collective-permute-start | bytes 6152 | tf_op jit(solution)/shard_map/while/body/eval_jaxpr/ppermute | solution.py:29
  110.7 4.0 %collective-permute-start = (f32[2,1,256]{2,1,0:T(1,128)S(1)}, f32[2,1,256]{2,1,0:T(1,128)S(1)}, u32[]{:S(2)}, u32[]{:S(2)}) collective-permute-start(f32[2,1,256]{2,1,0:T(1,128)S(1)} %get-tuple-element.333), channel_id=1, source_target_pairs={{1,0},{0,1},{3,2},{2,3},{5,4},{4,5},{7,6},{6,7},{9,8},{8,9},{11,10... | collective-permute-start | bytes 6152 | tf_op jit(solution)/shard_map/while/body/eval_jaxpr/ppermute | solution.py:30
  111.1 3.9 %collective-permute-start.1 = (f32[2,1,256]{2,1,0:T(1,128)S(1)}, f32[2,1,256]{2,1,0:T(1,128)S(1)}, u32[]{:S(2)}, u32[]{:S(2)}) collective-permute-start(f32[2,1,256]{2,1,0:T(1,128)S(1)} %get-tuple-element.334), channel_id=1, source_target_pairs={{0,1},{1,0},{2,3},{3,2},{4,5},{5,4},{6,7},{7,6},{8,9},{9,8},{10,11... | collective-permute-start | bytes 6152 | tf_op jit(solution)/shard_map/while/body/eval_jaxpr/ppermute | solution.py:29
  115.5 4.0 %collective-permute-start = (f32[2,1,256]{2,1,0:T(1,128)S(1)}, f32[2,1,256]{2,1,0:T(1,128)S(1)}, u32[]{:S(2)}, u32[]{:S(2)}) collective-permute-start(f32[2,1,256]{2,1,0:T(1,128)S(1)} %get-tuple-element.333), channel_id=1, source_target_pairs={{1,0},{0,1},{3,2},{2,3},{5,4},{4,5},{7,6},{6,7},{9,8},{8,9},{11,10... | collective-permute-start | bytes 6152 | tf_op jit(solution)/shard_map/while/body/eval_jaxpr/ppermute | solution.py:30
  118.3 3.9 %collective-permute-start.1 = (f32[2,1,256]{2,1,0:T(1,128)S(1)}, f32[2,1,256]{2,1,0:T(1,128)S(1)}, u32[]{:S(2)}, u32[]{:S(2)}) collective-permute-start(f32[2,1,256]{2,1,0:T(1,128)S(1)} %get-tuple-element.334), channel_id=1, source_target_pairs={{0,1},{1,0},{2,3},{3,2},{4,5},{5,4},{6,7},{7,6},{8,9},{9,8},{10,11... | collective-permute-start | bytes 6152 | tf_op jit(solution)/shard_map/while/body/eval_jaxpr/ppermute | solution.py:29
  122.7 4.0 %collective-permute-start = (f32[2,1,256]{2,1,0:T(1,128)S(1)}, f32[2,1,256]{2,1,0:T(1,128)S(1)}, u32[]{:S(2)}, u32[]{:S(2)}) collective-permute-start(f32[2,1,256]{2,1,0:T(1,128)S(1)} %get-tuple-element.333), channel_id=1, source_target_pairs={{1,0},{0,1},{3,2},{2,3},{5,4},{4,5},{7,6},{6,7},{9,8},{8,9},{11,10... | collective-permute-start | bytes 6152 | tf_op jit(solution)/shard_map/while/body/eval_jaxpr/ppermute | solution.py:30
  127.4 4.0 %collective-permute-start = (f32[2,1,256]{2,1,0:T(1,128)S(1)}, f32[2,1,256]{2,1,0:T(1,128)S(1)}, u32[]{:S(2)}, u32[]{:S(2)}) collective-permute-start(f32[2,1,256]{2,1,0:T(1,128)S(1)} %get-tuple-element.333), channel_id=1, source_target_pairs={{1,0},{0,1},{3,2},{2,3},{5,4},{4,5},{7,6},{6,7},{9,8},{8,9},{11,10... | collective-permute-start | bytes 6152 | tf_op jit(solution)/shard_map/while/body/eval_jaxpr/ppermute | solution.py:30
  134.7 4.0 %collective-permute-start = (f32[2,1,256]{2,1,0:T(1,128)S(1)}, f32[2,1,256]{2,1,0:T(1,128)S(1)}, u32[]{:S(2)}, u32[]{:S(2)}) collective-permute-start(f32[2,1,256]{2,1,0:T(1,128)S(1)} %get-tuple-element.333), channel_id=1, source_target_pairs={{1,0},{0,1},{3,2},{2,3},{5,4},{4,5},{7,6},{6,7},{9,8},{8,9},{11,10... | collective-permute-start | bytes 6152 | tf_op jit(solution)/shard_map/while/body/eval_jaxpr/ppermute | solution.py:30
  139.4 4.0 %collective-permute-start = (f32[2,1,256]{2,1,0:T(1,128)S(1)}, f32[2,1,256]{2,1,0:T(1,128)S(1)}, u32[]{:S(2)}, u32[]{:S(2)}) collective-permute-start(f32[2,1,256]{2,1,0:T(1,128)S(1)} %get-tuple-element.333), channel_id=1, source_target_pairs={{1,0},{0,1},{3,2},{2,3},{5,4},{4,5},{7,6},{6,7},{9,8},{8,9},{11,10... | collective-permute-start | bytes 6152 | tf_op jit(solution)/shard_map/while/body/eval_jaxpr/ppermute | solution.py:30
  146.6 4.0 %collective-permute-start = (f32[2,1,256]{2,1,0:T(1,128)S(1)}, f32[2,1,256]{2,1,0:T(1,128)S(1)}, u32[]{:S(2)}, u32[]{:S(2)}) collective-permute-start(f32[2,1,256]{2,1,0:T(1,128)S(1)} %get-tuple-element.333), channel_id=1, source_target_pairs={{1,0},{0,1},{3,2},{2,3},{5,4},{4,5},{7,6},{6,7},{9,8},{8,9},{11,10... | collective-permute-start | bytes 6152 | tf_op jit(solution)/shard_map/while/body/eval_jaxpr/ppermute | solution.py:30
  151.3 4.0 %collective-permute-start = (f32[2,1,256]{2,1,0:T(1,128)S(1)}, f32[2,1,256]{2,1,0:T(1,128)S(1)}, u32[]{:S(2)}, u32[]{:S(2)}) collective-permute-start(f32[2,1,256]{2,1,0:T(1,128)S(1)} %get-tuple-element.333), channel_id=1, source_target_pairs={{1,0},{0,1},{3,2},{2,3},{5,4},{4,5},{7,6},{6,7},{9,8},{8,9},{11,10... | collective-permute-start | bytes 6152 | tf_op jit(solution)/shard_map/while/body/eval_jaxpr/ppermute | solution.py:30
  154.2 4.0 %collective-permute-start.1 = (f32[2,1,256]{2,1,0:T(1,128)S(1)}, f32[2,1,256]{2,1,0:T(1,128)S(1)}, u32[]{:S(2)}, u32[]{:S(2)}) collective-permute-start(f32[2,1,256]{2,1,0:T(1,128)S(1)} %get-tuple-element.334), channel_id=1, source_target_pairs={{0,1},{1,0},{2,3},{3,2},{4,5},{5,4},{6,7},{7,6},{8,9},{9,8},{10,11... | collective-permute-start | bytes 6152 | tf_op jit(solution)/shard_map/while/body/eval_jaxpr/ppermute | solution.py:29
  158.6 4.0 %collective-permute-start = (f32[2,1,256]{2,1,0:T(1,128)S(1)}, f32[2,1,256]{2,1,0:T(1,128)S(1)}, u32[]{:S(2)}, u32[]{:S(2)}) collective-permute-start(f32[2,1,256]{2,1,0:T(1,128)S(1)} %get-tuple-element.333), channel_id=1, source_target_pairs={{1,0},{0,1},{3,2},{2,3},{5,4},{4,5},{7,6},{6,7},{9,8},{8,9},{11,10... | collective-permute-start | bytes 6152 | tf_op jit(solution)/shard_map/while/body/eval_jaxpr/ppermute | solution.py:30
  163.6 4.0 %collective-permute-start = (f32[2,1,256]{2,1,0:T(1,128)S(1)}, f32[2,1,256]{2,1,0:T(1,128)S(1)}, u32[]{:S(2)}, u32[]{:S(2)}) collective-permute-start(f32[2,1,256]{2,1,0:T(1,128)S(1)} %get-tuple-element.333), channel_id=1, source_target_pairs={{1,0},{0,1},{3,2},{2,3},{5,4},{4,5},{7,6},{6,7},{9,8},{8,9},{11,10... | collective-permute-start | bytes 6152 | tf_op jit(solution)/shard_map/while/body/eval_jaxpr/ppermute | solution.py:30
  170.5 4.0 %collective-permute-start = (f32[2,1,256]{2,1,0:T(1,128)S(1)}, f32[2,1,256]{2,1,0:T(1,128)S(1)}, u32[]{:S(2)}, u32[]{:S(2)}) collective-permute-start(f32[2,1,256]{2,1,0:T(1,128)S(1)} %get-tuple-element.333), channel_id=1, source_target_pairs={{1,0},{0,1},{3,2},{2,3},{5,4},{4,5},{7,6},{6,7},{9,8},{8,9},{11,10... | collective-permute-start | bytes 6152 | tf_op jit(solution)/shard_map/while/body/eval_jaxpr/ppermute | solution.py:30
  175.6 4.3 %collective-permute-start = (f32[2,1,256]{2,1,0:T(1,128)S(1)}, f32[2,1,256]{2,1,0:T(1,128)S(1)}, u32[]{:S(2)}, u32[]{:S(2)}) collective-permute-start(f32[2,1,256]{2,1,0:T(1,128)S(1)} %get-tuple-element.333), channel_id=1, source_target_pairs={{1,0},{0,1},{3,2},{2,3},{5,4},{4,5},{7,6},{6,7},{9,8},{8,9},{11,10... | collective-permute-start | bytes 6152 | tf_op jit(solution)/shard_map/while/body/eval_jaxpr/ppermute | solution.py:30
  182.5 4.0 %collective-permute-start = (f32[2,1,256]{2,1,0:T(1,128)S(1)}, f32[2,1,256]{2,1,0:T(1,128)S(1)}, u32[]{:S(2)}, u32[]{:S(2)}) collective-permute-start(f32[2,1,256]{2,1,0:T(1,128)S(1)} %get-tuple-element.333), channel_id=1, source_target_pairs={{1,0},{0,1},{3,2},{2,3},{5,4},{4,5},{7,6},{6,7},{9,8},{8,9},{11,10... | collective-permute-start | bytes 6152 | tf_op jit(solution)/shard_map/while/body/eval_jaxpr/ppermute | solution.py:30
  187.6 4.0 %collective-permute-start = (f32[2,1,256]{2,1,0:T(1,128)S(1)}, f32[2,1,256]{2,1,0:T(1,128)S(1)}, u32[]{:S(2)}, u32[]{:S(2)}) collective-permute-start(f32[2,1,256]{2,1,0:T(1,128)S(1)} %get-tuple-element.333), channel_id=1, source_target_pairs={{1,0},{0,1},{3,2},{2,3},{5,4},{4,5},{7,6},{6,7},{9,8},{8,9},{11,10... | collective-permute-start | bytes 6152 | tf_op jit(solution)/shard_map/while/body/eval_jaxpr/ppermute | solution.py:30
  190.0 4.2 %collective-permute-start.1 = (f32[2,1,256]{2,1,0:T(1,128)S(1)}, f32[2,1,256]{2,1,0:T(1,128)S(1)}, u32[]{:S(2)}, u32[]{:S(2)}) collective-permute-start(f32[2,1,256]{2,1,0:T(1,128)S(1)} %get-tuple-element.334), channel_id=1, source_target_pairs={{0,1},{1,0},{2,3},{3,2},{4,5},{5,4},{6,7},{7,6},{8,9},{9,8},{10,11... | collective-permute-start | bytes 6152 | tf_op jit(solution)/shard_map/while/body/eval_jaxpr/ppermute | solution.py:29
  194.7 4.0 %collective-permute-start = (f32[2,1,256]{2,1,0:T(1,128)S(1)}, f32[2,1,256]{2,1,0:T(1,128)S(1)}, u32[]{:S(2)}, u32[]{:S(2)}) collective-permute-start(f32[2,1,256]{2,1,0:T(1,128)S(1)} %get-tuple-element.333), channel_id=1, source_target_pairs={{1,0},{0,1},{3,2},{2,3},{5,4},{4,5},{7,6},{6,7},{9,8},{8,9},{11,10... | collective-permute-start | bytes 6152 | tf_op jit(solution)/shard_map/while/body/eval_jaxpr/ppermute | solution.py:30
  199.5 4.0 %collective-permute-start = (f32[2,1,256]{2,1,0:T(1,128)S(1)}, f32[2,1,256]{2,1,0:T(1,128)S(1)}, u32[]{:S(2)}, u32[]{:S(2)}) collective-permute-start(f32[2,1,256]{2,1,0:T(1,128)S(1)} %get-tuple-element.333), channel_id=1, source_target_pairs={{1,0},{0,1},{3,2},{2,3},{5,4},{4,5},{7,6},{6,7},{9,8},{8,9},{11,10... | collective-permute-start | bytes 6152 | tf_op jit(solution)/shard_map/while/body/eval_jaxpr/ppermute | solution.py:30
  206.6 4.0 %collective-permute-start = (f32[2,1,256]{2,1,0:T(1,128)S(1)}, f32[2,1,256]{2,1,0:T(1,128)S(1)}, u32[]{:S(2)}, u32[]{:S(2)}) collective-permute-start(f32[2,1,256]{2,1,0:T(1,128)S(1)} %get-tuple-element.333), channel_id=1, source_target_pairs={{1,0},{0,1},{3,2},{2,3},{5,4},{4,5},{7,6},{6,7},{9,8},{8,9},{11,10... | collective-permute-start | bytes 6152 | tf_op jit(solution)/shard_map/while/body/eval_jaxpr/ppermute | solution.py:30
  211.5 4.0 %collective-permute-start = (f32[2,1,256]{2,1,0:T(1,128)S(1)}, f32[2,1,256]{2,1,0:T(1,128)S(1)}, u32[]{:S(2)}, u32[]{:S(2)}) collective-permute-start(f32[2,1,256]{2,1,0:T(1,128)S(1)} %get-tuple-element.333), channel_id=1, source_target_pairs={{1,0},{0,1},{3,2},{2,3},{5,4},{4,5},{7,6},{6,7},{9,8},{8,9},{11,10... | collective-permute-start | bytes 6152 | tf_op jit(solution)/shard_map/while/body/eval_jaxpr/ppermute | solution.py:30
  214.2 4.0 %collective-permute-start.1 = (f32[2,1,256]{2,1,0:T(1,128)S(1)}, f32[2,1,256]{2,1,0:T(1,128)S(1)}, u32[]{:S(2)}, u32[]{:S(2)}) collective-permute-start(f32[2,1,256]{2,1,0:T(1,128)S(1)} %get-tuple-element.334), channel_id=1, source_target_pairs={{0,1},{1,0},{2,3},{3,2},{4,5},{5,4},{6,7},{7,6},{8,9},{9,8},{10,11... | collective-permute-start | bytes 6152 | tf_op jit(solution)/shard_map/while/body/eval_jaxpr/ppermute | solution.py:29
  218.6 4.0 %collective-permute-start = (f32[2,1,256]{2,1,0:T(1,128)S(1)}, f32[2,1,256]{2,1,0:T(1,128)S(1)}, u32[]{:S(2)}, u32[]{:S(2)}) collective-permute-start(f32[2,1,256]{2,1,0:T(1,128)S(1)} %get-tuple-element.333), channel_id=1, source_target_pairs={{1,0},{0,1},{3,2},{2,3},{5,4},{4,5},{7,6},{6,7},{9,8},{8,9},{11,10... | collective-permute-start | bytes 6152 | tf_op jit(solution)/shard_map/while/body/eval_jaxpr/ppermute | solution.py:30
  219.0 4.0 %collective-permute-start.1 = (f32[2,1,256]{2,1,0:T(1,128)S(1)}, f32[2,1,256]{2,1,0:T(1,128)S(1)}, u32[]{:S(2)}, u32[]{:S(2)}) collective-permute-start(f32[2,1,256]{2,1,0:T(1,128)S(1)} %get-tuple-element.334), channel_id=1, source_target_pairs={{0,1},{1,0},{2,3},{3,2},{4,5},{5,4},{6,7},{7,6},{8,9},{9,8},{10,11... | collective-permute-start | bytes 6152 | tf_op jit(solution)/shard_map/while/body/eval_jaxpr/ppermute | solution.py:29
  223.5 4.0 %collective-permute-start = (f32[2,1,256]{2,1,0:T(1,128)S(1)}, f32[2,1,256]{2,1,0:T(1,128)S(1)}, u32[]{:S(2)}, u32[]{:S(2)}) collective-permute-start(f32[2,1,256]{2,1,0:T(1,128)S(1)} %get-tuple-element.333), channel_id=1, source_target_pairs={{1,0},{0,1},{3,2},{2,3},{5,4},{4,5},{7,6},{6,7},{9,8},{8,9},{11,10... | collective-permute-start | bytes 6152 | tf_op jit(solution)/shard_map/while/body/eval_jaxpr/ppermute | solution.py:30
  230.6 4.0 %collective-permute-start = (f32[2,1,256]{2,1,0:T(1,128)S(1)}, f32[2,1,256]{2,1,0:T(1,128)S(1)}, u32[]{:S(2)}, u32[]{:S(2)}) collective-permute-start(f32[2,1,256]{2,1,0:T(1,128)S(1)} %get-tuple-element.333), channel_id=1, source_target_pairs={{1,0},{0,1},{3,2},{2,3},{5,4},{4,5},{7,6},{6,7},{9,8},{8,9},{11,10... | collective-permute-start | bytes 6152 | tf_op jit(solution)/shard_map/while/body/eval_jaxpr/ppermute | solution.py:30
  312.6 4.0 %collective-permute-start.11 = (f32[2,1,256]{2,1,0:T(1,128)S(1)}, f32[2,1,256]{2,1,0:T(1,128)S(1)}, u32[]{:S(2)}, u32[]{:S(2)}) collective-permute-start(f32[2,1,256]{2,1,0:T(1,128)S(1)} %get-tuple-element.220), channel_id=1, source_target_pairs={{0,1},{1,0},{2,3},{3,2},{4,5},{5,4},{6,7},{7,6},{8,9},{9,8},{10,11... | collective-permute-start | bytes 6152 | tf_op jit(solution)/shard_map/ppermute | solution.py:29
  315.5 3.9 %collective-permute-start.12 = (f32[2,1,256]{2,1,0:T(1,128)S(1)}, f32[2,1,256]{2,1,0:T(1,128)S(1)}, u32[]{:S(2)}, u32[]{:S(2)}) collective-permute-start(f32[2,1,256]{2,1,0:T(1,128)S(1)} %get-tuple-element.221), channel_id=1, source_target_pairs={{1,0},{0,1},{3,2},{2,3},{5,4},{4,5},{7,6},{6,7},{9,8},{8,9},{11,10... | collective-permute-start | bytes 6152 | tf_op jit(solution)/shard_map/ppermute | solution.py:30
  319.5 4.0 %collective-permute-start.13 = (f32[1,128,256]{2,1,0:T(8,128)S(1)}, f32[1,128,256]{2,1,0:T(8,128)S(1)}, u32[]{:S(2)}, u32[]{:S(2)}) collective-permute-start(f32[1,128,256]{2,1,0:T(8,128)S(1)} %get-tuple-element.218), channel_id=1, source_target_pairs={{0,2},{2,4},{4,6},{6,8},{8,10},{10,12},{12,14},{14,16},{16,18},{18... | collective-permute-start | bytes 393224 | tf_op jit(solution)/shard_map/ppermute | solution.py:37
  323.6 7.6 %collective-permute-start.14 = (f32[1,128,256]{2,1,0:T(8,128)S(1)}, f32[1,128,256]{2,1,0:T(8,128)S(1)}, u32[]{:S(2)}, u32[]{:S(2)}) collective-permute-start(f32[1,128,256]{2,1,0:T(8,128)S(1)} %get-tuple-element.217), channel_id=1, source_target_pairs={{0,254},{2,0},{4,2},{6,4},{8,6},{10,8},{12,10},{14,12},{16,14},{18... | collective-permute-start | bytes 393224 | tf_op jit(solution)/shard_map/ppermute | solution.py:37
  331.2 4.0 %collective-permute-start.15 = (f32[2,1,256]{2,1,0:T(1,128)S(1)}, f32[2,1,256]{2,1,0:T(1,128)S(1)}, u32[]{:S(2)}, u32[]{:S(2)}) collective-permute-start(f32[2,1,256]{2,1,0:T(1,128)S(1)} %get-tuple-element.214), channel_id=1, source_target_pairs={{0,1},{1,0},{2,3},{3,2},{4,5},{5,4},{6,7},{7,6},{8,9},{9,8},{10,11... | collective-permute-start | bytes 6152 | tf_op jit(solution)/shard_map/ppermute | solution.py:29
  (27 other events, 170.6 us)
where the time goes:
time: 340 us; the launch traced here: 338 us
  starting transfers between devices  124 us (36%)
  waiting for transfers between devices  103 us (30%)
  blocking collectives  72.8 us (21%)
  other arithmetic  17.5 us (5%)
  local copies, waits for them, and re-layouts  14.9 us (4%)
  matrix products  4.22 us (1%)
    all_to_all x1, blocking collectives, shards(): lax.all_to_all(accum, 'tm', split_axis=1, concat_axis=0, tiled=True)  53.4 us
    ppermute x29, starting transfers between devices, extended(): after = lax.ppermute(leading, axis, down)  43.9 us
    ppermute x29, starting transfers between devices, extended(): before = lax.ppermute(last, axis, up)  43 us
    ppermute x29, waiting for transfers between devices, extended(): before = lax.ppermute(last, axis, up)  40.5 us
    ppermute x29, waiting for transfers between devices, extended(): after = lax.ppermute(leading, axis, down)  22.6 us
    ppermute x5, starting transfers between devices, passed_along(): lax.ppermute(value, axis, [(i, (i + by) % size) for i in range(size)])  21 us
    all_to_all x1, blocking collectives, shards(): lax.all_to_all(mixed_back, 'tm', split_axis=0, concat_axis=1, tiled=True)  19.5 us
    all_to_all x1, waiting for transfers between devices, shards(): lax.all_to_all(residual, 'tm', split_axis=1, concat_axis=0, tiled=True)  14.3 us
  transfers between devices with their start and end apart: 65, of which 64 were waited for; matrix products, arithmetic and copies ran while one was open for 3% of the time, Pallas kernels for 0%

commit v1 on v0

v1 whole, which is shorter than its diff:
```python
import functools
import math

import jax
import jax.numpy as jnp
import numpy as np
from jax import lax
from jax.experimental import pallas as pl
from jax.experimental.pallas import tpu as pltpu
from jax.sharding import PartitionSpec as P

ORDER = 24
hop_angle = 0.3
coupling = 0.2
stiffness = 1.0
mass_term = 0.5
relaxation = 0.25
step_size = 0.25
cheb_base = 4.03
cheb_slope = 0.5
half_width = 4.0

MESH = pl.DeviceIdType.MESH
HIGHEST = lax.Precision.HIGHEST
PAD = 8
COSH = math.cosh(hop_angle)
SINH = math.sinh(hop_angle)


def time_basis(length):
    k = np.arange(length)[:, None]
    l = np.arange(length)[None, :]
    angle = ((2 * (k // 2) + 1) * l % (2 * length)) * (math.pi / length)
    return (math.sqrt(2.0 / length) * np.where(k % 2 == 0, np.cos(angle), np.sin(angle))).astype(np.float32)


def space_basis(length):
    k = np.arange(length)
    m = (k + 1) // 2
    angle = (m[:, None] * np.arange(length)[None, :] % length) * (2.0 * math.pi / length)
    basis = np.where((k % 2 == 1)[:, None], np.cos(angle), np.sin(angle)) * math.sqrt(2.0 / length)
    basis[0] = 1.0 / math.sqrt(length)
    basis[-1] = np.where(np.arange(length) % 2 == 0, 1.0, -1.0) / math.sqrt(length)
    return basis.astype(np.float32), (2.0 * np.cos(2.0 * math.pi * m / length))


def cheb_tables(length):
    m = np.arange(length) // 2
    centre = cheb_base + cheb_slope * (1.0 - np.cos((2 * m + 1) * math.pi / length))
    ratio = centre / half_width
    rows = [centre, 1.0 / centre]
    weight = 1.0 / ratio
    for _ in range(ORDER - 1):
        new = 1.0 / (2.0 * ratio - weight)
        rows += [new * weight, 2.0 * new / half_width]
        weight = new
    while len(rows) % 8:
        rows.append(np.zeros(length))
    return np.stack(rows).astype(np.float32)


def wrap(value, size):
    return jnp.where(value >= size, value - size, value)


def kernel(
    steps, phonon, momentum, source, guess, bonds, tbasis, sbasis, weights, lams, lamv, sol_out, mom_out,
    ext, bond_ext, tables, expo, poly, y, r, v, w, sol, ssem, rsem, hs, hr, own_sem,
):
    n, lat = steps, phonon.shape[2]
    rows = phonon.shape[1]
    total = rows + 2 * PAD
    tm, band = lax.axis_index("tm"), lax.axis_index("band")
    other = 1 - band
    me = 2 * tm + band
    after = wrap(tm + 1, n)
    before = jnp.where(tm == 0, n - 1, tm - 1)

    barrier = pltpu.get_barrier_semaphore()
    pl.semaphore_signal(barrier, inc=1, device_id=(tm, other), device_id_type=MESH)

    def greet(i, carry):
        t = wrap(tm + i, n)
        pl.semaphore_signal(barrier, inc=1, device_id=(t, band), device_id_type=MESH)
        pl.semaphore_signal(barrier, inc=1, device_id=(t, other), device_id_type=MESH)
        return carry

    lax.fori_loop(1, n, greet, 0)
    own = pl.ds(PAD, rows)
    for s in range(2):
        ext[0, 1 + s, own, :] = phonon[s]
        ext[1, 1 + s, own, :] = guess[s]
        bond_ext[s, own, :] = bonds[s]
    pl.semaphore_wait(barrier, 2 * n - 1)

    low, high = pl.ds(PAD - 2, 2), pl.ds(PAD + rows, 2)
    first, last = pl.ds(PAD, 2), pl.ds(PAD + rows - 2, 2)

    def send(j, src, dst, device):
        copy = pltpu.make_async_remote_copy(
            src_ref=src, dst_ref=dst, send_sem=hs.at[j], recv_sem=hr.at[j], device_id=device, device_id_type=MESH
        )
        copy.start()
        return copy

    both = pl.ds(0, 2)
    halo = [
        send(0, ext.at[both, 2, own], ext.at[both, 0, own], (after, band)),
        send(1, ext.at[1, 1, own], ext.at[1, 3, own], (before, band)),
        send(2, ext.at[both, pl.ds(1, 2), last], ext.at[both, pl.ds(1, 2), low], (tm, other)),
        send(3, ext.at[both, pl.ds(1, 2), first], ext.at[both, pl.ds(1, 2), high], (tm, other)),
        send(4, bond_ext.at[both, last], bond_ext.at[both, low], (tm, other)),
        send(5, bond_ext.at[both, first], bond_ext.at[both, high], (tm, other)),
        send(6, ext.at[both, 2, last], ext.at[both, 0, low], (after, other)),
        send(7, ext.at[both, 2, first], ext.at[both, 0, high], (after, other)),
        send(8, ext.at[1, 1, last], ext.at[1, 3, low], (before, other)),
        send(9, ext.at[1, 1, first], ext.at[1, 3, high], (before, other)),
        send(10, ext.at[0, 1, own], ext.at[0, 3, own], (before, band)),
    ]
    for copy in halo[:10]:
        copy.wait_recv()

    row_even = lax.broadcasted_iota(jnp.int32, (total, lat), 0) % 2 == 0
    col_even = lax.broadcasted_iota(jnp.int32, (total, lat), 1) % 2 == 0

    def rolled(value, by, axis):
        return pltpu.roll(value, by % value.shape[axis], axis)

    horizontal, vertical = bond_ext[0], bond_ext[1]
    left, up = rolled(horizontal, 1, 1), rolled(vertical, 1, 0)
    strengths = (
        jnp.where(col_even, horizontal, left),
        jnp.where(col_even, left, horizontal),
        jnp.where(row_even, vertical, up),
        jnp.where(row_even, up, vertical),
    )
    for q, s in enumerate(strengths):
        tables[2 * q] = jnp.where(s == 1, COSH, 1.0).astype(jnp.float32)
        tables[2 * q + 1] = jnp.where(s == 1, SINH, 0.0).astype(jnp.float32)

    def pairs(value, colours):
        for q in colours:
            axis, even = (1, col_even) if q < 2 else (0, row_even)
            plus, minus = rolled(value, -1, axis), rolled(value, 1, axis)
            partner = jnp.where(even, plus, minus) if q % 2 == 0 else jnp.where(even, minus, plus)
            value = tables[2 * q] * value + tables[2 * q + 1] * partner
        return value

    ahead = (0, 1, 2, 3)
    back = (3, 2, 1, 0)
    sign_before = jnp.where(tm == 0, -1.0, 1.0).astype(jnp.float32)
    sign_after = jnp.where(tm == n - 1, -1.0, 1.0).astype(jnp.float32)

    for s in range(3):
        expo[s] = jnp.exp(-coupling * ext[0, s])

    inner = slice(PAD, PAD + rows)
    link_own = guess[0] - pairs(expo[0] * (sign_before * ext[1, 0]), ahead)[inner]
    for s in range(2):
        applied = pairs(expo[1 + s] * ext[1, 1 + s], ahead)
        link = (ext[1, 2] if s == 0 else sign_after * ext[1, 3]) - applied
        pulled = pairs(link, back)[inner]
        residual = source[s] - (link_own - expo[1 + s, own, :] * pulled)
        link_own = link[inner]
        turned = lax.dot_general(
            sbasis[...], residual, (((1,), (1,)), ((), ())), precision=HIGHEST, preferred_element_type=jnp.float32
        )
        y[pl.ds(s, lat, 2), :] = turned

    def spread(k, src_of, dst, mine):
        ss, rs = ssem.at[k], rsem.at[k]

        def put(t, b):
            pltpu.make_async_remote_copy(
                src_ref=src_of(t, b), dst_ref=dst, send_sem=ss, recv_sem=rs, device_id=(t, b), device_id_type=MESH
            ).start()

        pltpu.make_async_copy(src_of(tm, band), dst, rs).start()
        put(tm, other)

        def body(i, carry):
            t = wrap(tm + i, n)
            put(t, band)
            put(t, other)
            return carry

        lax.fori_loop(1, n, body, 0)

    spread(0, lambda t, b: y.at[pl.ds(4 * t + 2 * b, 2)], r.at[band, pl.ds(2 * tm, 2)], None)

    lam_c = lamv[pl.ds(me, 1), :]
    chunk = 32

    def evaluate(i, carry):
        at = pl.ds(pl.multiple_of(i * chunk, chunk), chunk)
        lam_r = lams[at, :]
        shift = jnp.concatenate([lam_r + lam_c] * 2, axis=1)
        mu = weights[0:1, :] - shift
        direction = jnp.broadcast_to(weights[1:2, :], mu.shape)
        remaining = jnp.ones_like(mu)
        accum = jnp.zeros_like(mu)
        for step in range(ORDER):
            accum = accum + direction
            if step < ORDER - 1:
                remaining = remaining - mu * direction
                direction = weights[2 + 2 * step : 3 + 2 * step, :] * direction + weights[3 + 2 * step : 4 + 2 * step, :] * remaining
        poly[at, :] = relaxation * accum
        return carry

    lax.fori_loop(0, lat // chunk, evaluate, 0)
    pltpu.make_async_copy(r, r, rsem.at[0]).wait()

    def dot(a, b, ca, cb):
        return lax.dot_general(a, b, (((ca,), (cb,)), ((), ())), precision=HIGHEST, preferred_element_type=jnp.float32)

    spectrum = dot(sbasis[...], jnp.concatenate([r[0], r[1]], axis=1), 1, 1)
    spectrum = dot(spectrum, tbasis[...], 1, 1) * poly[...]
    timed = dot(spectrum, tbasis[...], 1, 0)
    timed = dot(timed, sbasis[...], 0, 0)
    v[0] = timed[:, :rows]
    v[1] = timed[:, rows:]
    spread(1, lambda t, b: v.at[b, pl.ds(2 * t, 2)], w.at[pl.ds(2 * me, 2)], None)
    pltpu.make_async_copy(w, w, rsem.at[1]).wait()

    halo2 = []

    def send2(j, src, dst, device):
        halo2.append(send(j, src, dst, device))

    for s in range(2):
        value = guess[s] + dot(w[pl.ds(s, lat, 2), :], sbasis[...], 0, 0)
        sol[s, own, :] = value
        sol_out[s] = value
        if s == 0:
            send2(11, sol.at[0, own], sol.at[2, own], (before, band))
            send2(12, sol.at[0, last], sol.at[2, low], (before, other))
            send2(13, sol.at[0, first], sol.at[2, high], (before, other))
    send2(14, sol.at[both, last], sol.at[both, low], (tm, other))
    send2(15, sol.at[both, first], sol.at[both, high], (tm, other))
    halo[10].wait_recv()
    for copy in halo2:
        copy.wait_recv()

    for s in range(2):
        applied = pairs(expo[1 + s] * sol[s], ahead)
        image = (sol[1] if s == 0 else sign_after * sol[2]) - applied
        pulled = pairs(image, back)[inner]
        fermion = (-2.0 * coupling) * expo[1 + s, own, :] * sol[s, own, :] * pulled
        here = phonon[s]
        boson = stiffness * (2.0 * here - ext[0, s, own, :] - ext[0, s + 2, own, :]) + mass_term * here
        mom_out[s] = momentum[s] - step_size * (boson + fermion)

    for copy in halo + halo2:
        copy.wait_send()
    for k in range(2):
        sent = w.at[pl.ds(0, 2 * (2 * n - 1))]
        pltpu.make_async_copy(sent, sent, ssem.at[k]).wait()


def shards(n, phonon, momentum, source, guess, bonds):
    slices, rows, lat = phonon.shape
    sbasis, lam = space_basis(lat)
    tbasis = time_basis(slices * n)
    weights = cheb_tables(slices * n)
    lams = np.ascontiguousarray(np.broadcast_to(lam.astype(np.float32)[:, None], (lat, 128)))
    vmem = pl.BlockSpec(memory_space=pltpu.VMEM)
    total = rows + 2 * PAD
    f32 = jnp.float32
    return pl.pallas_call(
        functools.partial(kernel, n),
        out_shape=[jax.ShapeDtypeStruct(phonon.shape, f32)] * 2,
        in_specs=[vmem] * 10,
        out_specs=[vmem] * 2,
        scratch_shapes=[
            pltpu.VMEM((2, 4, total, lat), f32),
            pltpu.VMEM((2, total, lat), jnp.int32),
            pltpu.VMEM((8, total, lat), f32),
            pltpu.VMEM((3, total, lat), f32),
            pltpu.VMEM((lat, lat), f32),
            pltpu.VMEM((2 * lat, rows), f32),
            pltpu.VMEM((2, slices * n, rows), f32),
            pltpu.VMEM((2, slices * n, rows), f32),
            pltpu.VMEM((2 * lat, rows), f32),
            pltpu.VMEM((3, total, lat), f32),
            pltpu.SemaphoreType.DMA((2,)),
            pltpu.SemaphoreType.DMA((2,)),
            pltpu.SemaphoreType.DMA((16,)),
            pltpu.SemaphoreType.DMA((16,)),
            pltpu.SemaphoreType.DMA,
        ],
        compiler_params=pltpu.CompilerParams(
            collective_id=0, has_side_effects=True, vmem_limit_bytes=32 * 1024 * 1024
        ),
        cost_estimate=pl.CostEstimate(flops=400000000, bytes_accessed=3000000, transcendentals=200000),
    )(phonon, momentum, source, guess, bonds, jnp.asarray(tbasis), jnp.asarray(sbasis), jnp.asarray(weights), jnp.asarray(lams), jnp.asarray(lams))


def solution(mesh):
    spec = P("tm", "band", None)
    return jax.shard_map(
        functools.partial(shards, mesh.shape["tm"]),
        mesh=mesh,
        in_specs=(spec, spec, spec, spec, P(None, "band", None)),
        out_specs=(spec, spec),
        check_vma=False,
    )
```

time: 340 us -> 64.1 us (0.19)
  starting transfers between devices: 124 us -> 0 us
  waiting for transfers between devices: 103 us -> 0 us
  blocking collectives: 72.8 us -> 0 us
  Pallas kernels: 0 us -> 53.3 us
  other arithmetic: 17.5 us -> 0 us
  local copies, waits for them, and re-layouts: 14.9 us -> 9.75 us
  matrix products: 4.22 us -> 0 us
    ppermute x63 -> x0, starting transfers between devices: 108 us -> none  [the longest x29 43.9 us: extended(): after = lax.ppermute(leading, axis, down)]
    ppermute x63 -> x0, waiting for transfers between devices: 74 us -> none  [the longest x29 40.5 us: extended(): before = lax.ppermute(last, axis, up)]
    all_to_all x2 -> x0, blocking collectives: 72.8 us -> none  [the longest x1 53.4 us: shards(): lax.all_to_all(accum, 'tm', split_axis=1, concat_axis=0, tiled=True)]
    pallas_call x0 -> x1, Pallas kernels: none -> 53.3 us  [shards(): pl.pallas_call(functools.partial(kernel, n), out_shape=[jax.ShapeDtypeStr...]
    all_to_all x2 -> x0, waiting for transfers between devices: 28.5 us -> none  [the longest x1 14.3 us: shards(): lax.all_to_all(residual, 'tm', split_axis=1, concat_axis=0, tiled=True)]
    all_to_all x2 -> x0, starting transfers between devices: 15.5 us -> none  [the longest x1 9.86 us: shards(): lax.all_to_all(residual, 'tm', split_axis=1, concat_axis=0, tiled=True)]
    add x39 -> x0, other arithmetic: 11.7 us -> none  [the longest x24 9.75 us: sweep_each(): weight_new * weight_now * direction]
    slice x106 -> x0, local copies, waits for them, and re-layouts: 9.28 us -> none  [the longest x48 5.38 us: sweep_each(): jnp.roll(direction, 1, 2)]
  transfers between devices with their start and end apart: 65 -> 0, of which waited for: 64 -> 0; matrix products, arithmetic and copies ran while one was open for 3% -> 0% of each run, Pallas kernels for 0% -> 0%
where the time goes in v1:
time: 64.1 us; the launch traced here: 63.7 us
  Pallas kernels  53.3 us (83%)
  local copies, waits for them, and re-layouts  9.75 us (15%)
  between operations  0.66 us (1%)
    pallas_call x1, Pallas kernels, shards(): pl.pallas_call(functools.partial(kernel, n), out_shape=[jax.ShapeDtypeStr...  53.3 us
    unnamed x20, local copies, waits for them, and re-layouts  9.75 us

profile of v1, /device:TPU:1, one launch (start us, length us, event | category | flops | bytes accessed | tf_op | source)
XLA Modules:
  0.0 63.7 jit_solution(11531582509856835914)
XLA Ops:
  0.6 0.0 copy-start
  0.6 0.9 %copy-done = f32[256,128]{1,0:T(8,128)S(1)} copy-done((f32[256,128]{1,0:T(8,128)S(1)}, f32[256,128]{1,0:T(8,128)}, u32[]{:S(2)}) %copy-start) | copy-done | bytes 131096
  1.5 0.0 copy-start.1
  1.5 0.9 %copy-done.1 = f32[2,128,256]{2,1,0:T(8,128)S(1)} copy-done((f32[2,128,256]{2,1,0:T(8,128)S(1)}, f32[2,128,256]{2,1,0:T(8,128)}, u32[]{:S(2)}) %copy-start.1) | copy-done | bytes 262168
  2.5 0.0 copy-start.2
  2.5 0.9 %copy-done.2 = f32[2,128,256]{2,1,0:T(8,128)S(1)} copy-done((f32[2,128,256]{2,1,0:T(8,128)S(1)}, f32[2,128,256]{2,1,0:T(8,128)}, u32[]{:S(2)}) %copy-start.2) | copy-done | bytes 262168
  3.4 0.0 copy-start.3
  3.4 0.9 %copy-done.3 = f32[2,128,256]{2,1,0:T(8,128)S(1)} copy-done((f32[2,128,256]{2,1,0:T(8,128)S(1)}, f32[2,128,256]{2,1,0:T(8,128)}, u32[]{:S(2)}) %copy-start.3) | copy-done | bytes 262168
  4.4 0.0 copy-start.4
  4.4 0.9 %copy-done.4 = f32[2,128,256]{2,1,0:T(8,128)S(1)} copy-done((f32[2,128,256]{2,1,0:T(8,128)S(1)}, f32[2,128,256]{2,1,0:T(8,128)}, u32[]{:S(2)}) %copy-start.4) | copy-done | bytes 262168
  5.3 0.0 copy-start.5
  5.3 0.9 %copy-done.5 = s32[2,128,256]{2,1,0:T(8,128)S(1)} copy-done((s32[2,128,256]{2,1,0:T(8,128)S(1)}, s32[2,128,256]{2,1,0:T(8,128)}, u32[]{:S(2)}) %copy-start.5) | copy-done | bytes 262168
  6.3 0.0 copy-start.6
  6.3 0.9 %copy-done.6 = f32[256,256]{1,0:T(8,128)S(1)} copy-done((f32[256,256]{1,0:T(8,128)S(1)}, f32[256,256]{1,0:T(8,128)}, u32[]{:S(2)}) %copy-start.6) | copy-done | bytes 262168
  7.2 0.0 copy-start.7
  7.2 0.9 %copy-done.7 = f32[256,256]{1,0:T(8,128)S(1)} copy-done((f32[256,256]{1,0:T(8,128)S(1)}, f32[256,256]{1,0:T(8,128)}, u32[]{:S(2)}) %copy-start.7) | copy-done | bytes 262168
  8.2 0.0 copy-start.8
  8.2 0.8 %copy-done.8 = f32[48,256]{1,0:T(8,128)S(1)} copy-done((f32[48,256]{1,0:T(8,128)S(1)}, f32[48,256]{1,0:T(8,128)}, u32[]{:S(2)}) %copy-start.8) | copy-done | bytes 49176
  9.0 53.3 %shard_map.104 = (f32[2,128,256]{2,1,0:T(8,128)S(1)}, f32[2,128,256]{2,1,0:T(8,128)S(1)}) custom-call(f32[2,128,256]{2,1,0:T(8,128)S(1)} %copy-done.1, f32[2,128,256]{2,1,0:T(8,128)S(1)} %copy-done.2, f32[2,128,256]{2,1,0:T(8,128)S(1)} %copy-done.3, f32[2,128,256]{2,1,0:T(8,128)S(1)} %copy-done.4, s32[2,128,256]{2,1,0:T(8,128)S(1)} %copy-done.5, ...), custom_call_target="tpu_custom_call" | custom-call | flops 400000000 | bytes 3000000 | tf_op jit(solution)/shard_map/pallas_call | solution.py:269
  62.3 0.7 %copy.13 = f32[2,128,256]{2,1,0:T(8,128)} copy(f32[2,128,256]{2,1,0:T(8,128)S(1)} %get-tuple-element.4) | data formatting | bytes 524288
  63.0 0.7 %copy.14 = f32[2,128,256]{2,1,0:T(8,128)} copy(f32[2,128,256]{2,1,0:T(8,128)S(1)} %get-tuple-element.5) | data formatting | bytes 524288
Async XLA Ops:
  0.6 0.9 %copy-start = (f32[256,128]{1,0:T(8,128)S(1)}, f32[256,128]{1,0:T(8,128)}, u32[]{:S(2)}) copy-start(f32[256,128]{1,0:T(8,128)} %constant.11.clone.lams.lamv) | copy-start | bytes 393220
  1.5 0.9 %copy-start.1 = (f32[2,128,256]{2,1,0:T(8,128)S(1)}, f32[2,128,256]{2,1,0:T(8,128)}, u32[]{:S(2)}) copy-start(f32[2,128,256]{2,1,0:T(8,128)} %phonon.1) | copy-start | bytes 786436
  2.5 0.9 %copy-start.2 = (f32[2,128,256]{2,1,0:T(8,128)S(1)}, f32[2,128,256]{2,1,0:T(8,128)}, u32[]{:S(2)}) copy-start(f32[2,128,256]{2,1,0:T(8,128)} %momentum.1) | copy-start | bytes 786436
  3.4 0.9 %copy-start.3 = (f32[2,128,256]{2,1,0:T(8,128)S(1)}, f32[2,128,256]{2,1,0:T(8,128)}, u32[]{:S(2)}) copy-start(f32[2,128,256]{2,1,0:T(8,128)} %source.1) | copy-start | bytes 786436
  4.4 0.9 %copy-start.4 = (f32[2,128,256]{2,1,0:T(8,128)S(1)}, f32[2,128,256]{2,1,0:T(8,128)}, u32[]{:S(2)}) copy-start(f32[2,128,256]{2,1,0:T(8,128)} %guess.1) | copy-start | bytes 786436
  5.3 0.9 %copy-start.5 = (s32[2,128,256]{2,1,0:T(8,128)S(1)}, s32[2,128,256]{2,1,0:T(8,128)}, u32[]{:S(2)}) copy-start(s32[2,128,256]{2,1,0:T(8,128)} %bonds.1) | copy-start | bytes 786436
  6.3 0.9 %copy-start.6 = (f32[256,256]{1,0:T(8,128)S(1)}, f32[256,256]{1,0:T(8,128)}, u32[]{:S(2)}) copy-start(f32[256,256]{1,0:T(8,128)} %constant.9.clone.sbasis) | copy-start | bytes 786436
  7.2 0.9 %copy-start.7 = (f32[256,256]{1,0:T(8,128)S(1)}, f32[256,256]{1,0:T(8,128)}, u32[]{:S(2)}) copy-start(f32[256,256]{1,0:T(8,128)} %constant.8.clone.tbasis) | copy-start | bytes 786436
  8.2 0.8 %copy-start.8 = (f32[48,256]{1,0:T(8,128)S(1)}, f32[48,256]{1,0:T(8,128)}, u32[]{:S(2)}) copy-start(f32[48,256]{1,0:T(8,128)} %constant.10.clone.weights) | copy-start | bytes 147460

commit v2 on v1

--- a/solution.py
+++ b/solution.py
@@ -20,6 +20,7 @@
 cheb_slope = 0.5
 half_width = 4.0
 
+STRIDE = 1
 MESH = pl.DeviceIdType.MESH
 HIGHEST = lax.Precision.HIGHEST
 PAD = 8
@@ -64,35 +65,63 @@
 
 
 def kernel(
-    steps, phonon, momentum, source, guess, bonds, tbasis, sbasis, weights, lams, lamv, sol_out, mom_out,
-    ext, bond_ext, tables, expo, poly, y, r, v, w, sol, ssem, rsem, hs, hr, own_sem,
+    n, phonon_in, momentum_in, source_in, guess_in, bonds_in, tbasis_in, sbasis_in, weights_in, lams_in, sol_out, mom_out,
+    source, momentum, tbasis, sbasis, weights, lams,
+    ext, bond_ext, tables, expo, poly, y, r, v, w, sol, ssem, rsem, hs, hr, loads, far,
 ):
-    n, lat = steps, phonon.shape[2]
-    rows = phonon.shape[1]
+    rows, lat = source.shape[1:]
     total = rows + 2 * PAD
     tm, band = lax.axis_index("tm"), lax.axis_index("band")
     other = 1 - band
     me = 2 * tm + band
     after = wrap(tm + 1, n)
     before = jnp.where(tm == 0, n - 1, tm - 1)
-
+    own = pl.ds(PAD, rows)
+    both = pl.ds(0, 2)
+
+    def load(j, src, dst):
+        copy = pltpu.make_async_copy(src, dst, loads.at[j])
+        copy.start()
+        return copy
+
+    load_first = [
+        load(0, guess_in, ext.at[1, pl.ds(1, 2), own]),
+        load(1, phonon_in, ext.at[0, pl.ds(1, 2), own]),
+        load(2, bonds_in, bond_ext.at[both, own]),
+    ]
+
+    near = 8
+    count = n // near
+    row, col = tm // near, tm % near
     barrier = pltpu.get_barrier_semaphore()
-    pl.semaphore_signal(barrier, inc=1, device_id=(tm, other), device_id_type=MESH)
-
-    def greet(i, carry):
-        t = wrap(tm + i, n)
-        pl.semaphore_signal(barrier, inc=1, device_id=(t, band), device_id_type=MESH)
-        pl.semaphore_signal(barrier, inc=1, device_id=(t, other), device_id_type=MESH)
-        return carry
-
-    lax.fori_loop(1, n, greet, 0)
-    own = pl.ds(PAD, rows)
-    for s in range(2):
-        ext[0, 1 + s, own, :] = phonon[s]
-        ext[1, 1 + s, own, :] = guess[s]
-        bond_ext[s, own, :] = bonds[s]
-    pl.semaphore_wait(barrier, 2 * n - 1)
-
+
+    def signal(sem, t, b):
+        pl.semaphore_signal(sem, inc=1, device_id=(t, b), device_id_type=MESH)
+
+    def far_signals(sem):
+        for i in range(1, count):
+            signal(sem, wrap(row + i, count) * near + col, band)
+
+    for t in (after, before):
+        signal(barrier, t, band)
+        signal(barrier, t, other)
+    signal(barrier, tm, other)
+    for i in range(1, near):
+        t = row * near + wrap(col + i, near)
+        signal(barrier, t, band)
+        signal(barrier, t, other)
+    far_signals(barrier)
+    load_later = [
+        load(3, source_in, source),
+        load(4, sbasis_in, sbasis),
+        load(5, tbasis_in, tbasis),
+        load(6, weights_in, weights),
+        load(7, lams_in, lams),
+        load(8, momentum_in, momentum),
+    ]
+    for copy in load_first:
+        copy.wait()
+    pl.semaphore_wait(barrier, 5 + 2 * (near - 1) + count - 1)
     low, high = pl.ds(PAD - 2, 2), pl.ds(PAD + rows, 2)
     first, last = pl.ds(PAD, 2), pl.ds(PAD + rows - 2, 2)
 
@@ -103,7 +132,6 @@
         copy.start()
         return copy
 
-    both = pl.ds(0, 2)
     halo = [
         send(0, ext.at[both, 2, own], ext.at[both, 0, own], (after, band)),
         send(1, ext.at[1, 1, own], ext.at[1, 3, own], (before, band)),
@@ -117,9 +145,9 @@
         send(9, ext.at[1, 1, first], ext.at[1, 3, high], (before, other)),
         send(10, ext.at[0, 1, own], ext.at[0, 3, own], (before, band)),
     ]
+    far_signals(far)
     for copy in halo[:10]:
         copy.wait_recv()
-
     row_even = lax.broadcasted_iota(jnp.int32, (total, lat), 0) % 2 == 0
     col_even = lax.broadcasted_iota(jnp.int32, (total, lat), 1) % 2 == 0
 
@@ -154,8 +182,10 @@
     for s in range(3):
         expo[s] = jnp.exp(-coupling * ext[0, s])
 
+    for copy in load_later[:2]:
+        copy.wait()
     inner = slice(PAD, PAD + rows)
-    link_own = guess[0] - pairs(expo[0] * (sign_before * ext[1, 0]), ahead)[inner]
+    link_own = ext[1, 1, own, :] - pairs(expo[0] * (sign_before * ext[1, 0]), ahead)[inner]
     for s in range(2):
         applied = pairs(expo[1 + s] * ext[1, 1 + s], ahead)
         link = (ext[1, 2] if s == 0 else sign_after * ext[1, 3]) - applied
@@ -167,7 +197,8 @@
         )
         y[pl.ds(s, lat, 2), :] = turned
 
-    def spread(k, src_of, dst, mine):
+    pl.semaphore_wait(far, count - 1)
+    def spread(k, src_of, dst):
         ss, rs = ssem.at[k], rsem.at[k]
 
         def put(t, b):
@@ -179,16 +210,18 @@
         put(tm, other)
 
         def body(i, carry):
-            t = wrap(tm + i, n)
+            t = wrap(tm + carry, n)
             put(t, band)
             put(t, other)
-            return carry
-
-        lax.fori_loop(1, n, body, 0)
-
-    spread(0, lambda t, b: y.at[pl.ds(4 * t + 2 * b, 2)], r.at[band, pl.ds(2 * tm, 2)], None)
-
-    lam_c = lamv[pl.ds(me, 1), :]
+            return wrap(carry + STRIDE, n)
+
+        lax.fori_loop(1, n, body, STRIDE)
+
+    spread(0, lambda t, b: y.at[pl.ds(4 * t + 2 * b, 2)], r.at[band, pl.ds(2 * tm, 2)])
+
+    for copy in load_later[2:]:
+        copy.wait()
+    lam_c = lams[pl.ds(me, 1), :]
     chunk = 32
 
     def evaluate(i, carry):
@@ -219,7 +252,7 @@
     timed = dot(timed, sbasis[...], 0, 0)
     v[0] = timed[:, :rows]
     v[1] = timed[:, rows:]
-    spread(1, lambda t, b: v.at[b, pl.ds(2 * t, 2)], w.at[pl.ds(2 * me, 2)], None)
+    spread(1, lambda t, b: v.at[b, pl.ds(2 * t, 2)], w.at[pl.ds(2 * me, 2)])
     pltpu.make_async_copy(w, w, rsem.at[1]).wait()
 
     halo2 = []
@@ -228,7 +261,7 @@
         halo2.append(send(j, src, dst, device))
 
     for s in range(2):
-        value = guess[s] + dot(w[pl.ds(s, lat, 2), :], sbasis[...], 0, 0)
+        value = ext[1, 1 + s, own, :] + dot(w[pl.ds(s, lat, 2), :], sbasis[...], 0, 0)
         sol[s, own, :] = value
         sol_out[s] = value
         if s == 0:
@@ -246,7 +279,7 @@
         image = (sol[1] if s == 0 else sign_after * sol[2]) - applied
         pulled = pairs(image, back)[inner]
         fermion = (-2.0 * coupling) * expo[1 + s, own, :] * sol[s, own, :] * pulled
-        here = phonon[s]
+        here = ext[0, 1 + s, own, :]
         boson = stiffness * (2.0 * here - ext[0, s, own, :] - ext[0, s + 2, own, :]) + mass_term * here
         mom_out[s] = momentum[s] - step_size * (boson + fermion)
 
@@ -264,14 +297,21 @@
     weights = cheb_tables(slices * n)
     lams = np.ascontiguousarray(np.broadcast_to(lam.astype(np.float32)[:, None], (lat, 128)))
     vmem = pl.BlockSpec(memory_space=pltpu.VMEM)
+    hbm = pl.BlockSpec(memory_space=pltpu.HBM)
     total = rows + 2 * PAD
     f32 = jnp.float32
     return pl.pallas_call(
         functools.partial(kernel, n),
         out_shape=[jax.ShapeDtypeStruct(phonon.shape, f32)] * 2,
-        in_specs=[vmem] * 10,
+        in_specs=[hbm] * 9,
         out_specs=[vmem] * 2,
         scratch_shapes=[
+            pltpu.VMEM(phonon.shape, f32),
+            pltpu.VMEM(phonon.shape, f32),
+            pltpu.VMEM(tbasis.shape, f32),
+            pltpu.VMEM(sbasis.shape, f32),
+            pltpu.VMEM(weights.shape, f32),
+            pltpu.VMEM(lams.shape, f32),
             pltpu.VMEM((2, 4, total, lat), f32),
             pltpu.VMEM((2, total, lat), jnp.int32),
             pltpu.VMEM((8, total, lat), f32),
@@ -286,17 +326,18 @@
             pltpu.SemaphoreType.DMA((2,)),
             pltpu.SemaphoreType.DMA((16,)),
             pltpu.SemaphoreType.DMA((16,)),
-            pltpu.SemaphoreType.DMA,
+            pltpu.SemaphoreType.DMA((9,)),
+            pltpu.SemaphoreType.REGULAR,
         ],
         compiler_params=pltpu.CompilerParams(
-            collective_id=0, has_side_effects=True, vmem_limit_bytes=32 * 1024 * 1024
+            collective_id=0, has_side_effects=True, vmem_limit_bytes=63 * 1024 * 1024
         ),
         cost_estimate=pl.CostEstimate(flops=400000000, bytes_accessed=3000000, transcendentals=200000),
-    )(phonon, momentum, source, guess, bonds, jnp.asarray(tbasis), jnp.asarray(sbasis), jnp.asarray(weights), jnp.asarray(lams), jnp.asarray(lams))
+    )(phonon, momentum, source, guess, bonds, jnp.asarray(tbasis), jnp.asarray(sbasis), jnp.asarray(weights), jnp.asarray(lams))
 
 
 def solution(mesh):
-    spec = P("tm", "band", None)
+    spec = P("tm", "band")
     return jax.shard_map(
         functools.partial(shards, mesh.shape["tm"]),
         mesh=mesh,

time: 64.1 us -> 54.8 us (0.85)
  local copies, waits for them, and re-layouts: 9.75 us -> 2.42 us
  Pallas kernels: 53.3 us -> 51.6 us
    unnamed x20 -> x4, local copies, waits for them, and re-layouts: 9.75 us -> 2.42 us
    pallas_call x1, Pallas kernels: 53.3 us -> 51.6 us  [shards(): pl.pallas_call(functools.partial(kernel, n), out_shape=[jax.ShapeDtypeStr...]
where the time goes in v2:
time: 54.8 us; the launch traced here: 54.7 us
  Pallas kernels  51.6 us (94%)
  local copies, waits for them, and re-layouts  2.42 us (4%)
  between operations  0.65 us (1%)
    pallas_call x1, Pallas kernels, shards(): pl.pallas_call(functools.partial(kernel, n), out_shape=[jax.ShapeDtypeStr...  51.6 us
    unnamed x4, local copies, waits for them, and re-layouts  2.42 us

profile of v2, /device:TPU:1, one launch (start us, length us, event | category | flops | bytes accessed | tf_op | source)
XLA Modules:
  0.0 54.7 jit_solution(14664913329830668136)
XLA Ops:
  0.6 51.6 %shard_map.104 = (f32[2,128,256]{2,1,0:T(8,128)}, f32[2,128,256]{2,1,0:T(8,128)}) custom-call(f32[2,128,256]{2,1,0:T(8,128)} %phonon_in.1, f32[2,128,256]{2,1,0:T(8,128)} %momentum_in.1, f32[2,128,256]{2,1,0:T(8,128)} %source_in.1, f32[2,128,256]{2,1,0:T(8,128)} %guess_in.1, s32[2,128,256]{2,1,0:T(8,128)} %bonds_in.1, f32[256,256]{1,0:T(8,128)} %constant.8.clone.tbasis_in, ...), custom_call_target="tpu_custom_call" | custom-call | flops 400000000 | bytes 3000000 | tf_op jit(solution)/shard_map/pallas_call | solution.py:303
  52.2 0.0 copy-start
  52.2 1.7 %copy.13 = f32[2,128,256]{2,1,0:T(8,128)} copy(f32[2,128,256]{2,1,0:T(8,128)} %get-tuple-element.4) | data formatting | bytes 524288
  54.0 0.0 copy-done
  54.0 0.7 %copy.14 = f32[2,128,256]{2,1,0:T(8,128)} copy(f32[2,128,256]{2,1,0:T(8,128)S(1)} %copy-done) | data formatting | bytes 524288
Async XLA Ops:
  52.2 1.7 %copy-start = (f32[2,128,256]{2,1,0:T(8,128)S(1)}, f32[2,128,256]{2,1,0:T(8,128)}, u32[]{:S(2)}) copy-start(f32[2,128,256]{2,1,0:T(8,128)} %get-tuple-element.5) | copy-start | bytes 786436

commit v3 on v2

v3 whole, which is shorter than its diff:
```python
import functools
import math

import jax
import jax.numpy as jnp
import numpy as np
from jax import lax
from jax.experimental import pallas as pl
from jax.experimental.pallas import tpu as pltpu
from jax.sharding import PartitionSpec as P

ORDER = 24
hop_angle = 0.3
coupling = 0.2
stiffness = 1.0
mass_term = 0.5
relaxation = 0.25
step_size = 0.25
cheb_base = 4.03
cheb_slope = 0.5
half_width = 4.0

MESH = pl.DeviceIdType.MESH
PAD = 8
COSH = math.cosh(hop_angle)
SINH = math.sinh(hop_angle)


def time_basis(length):
    k = np.arange(length)[:, None]
    l = np.arange(length)[None, :]
    angle = ((2 * (k // 2) + 1) * l % (2 * length)) * (math.pi / length)
    return (math.sqrt(2.0 / length) * np.where(k % 2 == 0, np.cos(angle), np.sin(angle))).astype(np.float32)


def space_basis(length):
    k = np.arange(length)
    m = (k + 1) // 2
    angle = (m[:, None] * np.arange(length)[None, :] % length) * (2.0 * math.pi / length)
    basis = np.where((k % 2 == 1)[:, None], np.cos(angle), np.sin(angle)) * math.sqrt(2.0 / length)
    basis[0] = 1.0 / math.sqrt(length)
    basis[-1] = np.where(np.arange(length) % 2 == 0, 1.0, -1.0) / math.sqrt(length)
    return basis.astype(np.float32), (2.0 * np.cos(2.0 * math.pi * m / length))


def cheb_tables(length):
    m = np.arange(length) // 2
    centre = cheb_base + cheb_slope * (1.0 - np.cos((2 * m + 1) * math.pi / length))
    ratio = centre / half_width
    rows = [centre, 1.0 / centre]
    weight = 1.0 / ratio
    for _ in range(ORDER - 1):
        new = 1.0 / (2.0 * ratio - weight)
        rows += [new * weight, 2.0 * new / half_width]
        weight = new
    while len(rows) % 8:
        rows.append(np.zeros(length))
    return np.stack(rows).astype(np.float32)


def wrap(value, size):
    return jnp.where(value >= size, value - size, value)


def halves(value):
    top = value.astype(jnp.bfloat16)
    return top, (value - top.astype(jnp.float32)).astype(jnp.bfloat16)


def dot(a, b, ca, cb):
    dims = (((ca,), (cb,)), ((), ()))

    def one(p, q):
        return lax.dot_general(p, q, dims, preferred_element_type=jnp.float32)

    return one(a[0], b[0]) + (one(a[0], b[1]) + one(a[1], b[0]))


def kernel(
    n, phonon_in, momentum_in, source_in, guess_in, bonds_in, tbasis_in, sbasis_in, weights_in, lams_in, sol_out, mom_out,
    source, momentum, tbasis, sbasis, weights, lams,
    ext, bond_ext, tables, expo, app, app_in, app_edge, edge_out, phonon_prev, poly, y, r, v, w, sol, new,
    ssem, rsem, hs, hr, loads, far,
):
    rows, lat = source.shape[1:]
    total = rows + 2 * PAD
    tm, band = lax.axis_index("tm"), lax.axis_index("band")
    other = 1 - band
    me = 2 * tm + band
    after = wrap(tm + 1, n)
    before = jnp.where(tm == 0, n - 1, tm - 1)
    own = pl.ds(PAD, rows)
    both = pl.ds(0, 2)

    def load(j, src, dst):
        copy = pltpu.make_async_copy(src, dst, loads.at[j])
        copy.start()
        return copy

    load_first = [
        load(0, guess_in, ext.at[1, both, own]),
        load(1, phonon_in, ext.at[0, both, own]),
        load(2, bonds_in, bond_ext.at[both, own]),
    ]

    near = 8
    count = n // near
    row, col = tm // near, tm % near
    barrier = pltpu.get_barrier_semaphore()

    def signal(sem, t, b):
        pl.semaphore_signal(sem, inc=1, device_id=(t, b), device_id_type=MESH)

    def far_signals(sem):
        for i in range(1, count):
            signal(sem, wrap(row + i, count) * near + col, band)

    for t in (after, before):
        signal(barrier, t, band)
        signal(barrier, t, other)
    signal(barrier, tm, other)
    for i in range(1, near):
        t = row * near + wrap(col + i, near)
        signal(barrier, t, band)
        signal(barrier, t, other)
    far_signals(barrier)
    load_later = [
        load(3, source_in, source),
        load(4, sbasis_in, sbasis),
        load(5, tbasis_in, tbasis),
        load(6, weights_in, weights),
        load(7, lams_in, lams),
        load(8, momentum_in, momentum),
    ]
    for copy in load_first:
        copy.wait()
    pl.semaphore_wait(barrier, 5 + 2 * (near - 1) + count - 1)
    low, high = pl.ds(PAD - 2, 2), pl.ds(PAD + rows, 2)
    first, last = pl.ds(PAD, 2), pl.ds(PAD + rows - 2, 2)
    started = []

    def send(j, src, dst, device):
        copy = pltpu.make_async_remote_copy(
            src_ref=src, dst_ref=dst, send_sem=hs.at[j], recv_sem=hr.at[j], device_id=device, device_id_type=MESH
        )
        copy.start()
        started.append(copy)
        return copy

    edges = [
        send(1, ext.at[both, both, last], ext.at[both, both, low], (tm, other)),
        send(2, ext.at[both, both, first], ext.at[both, both, high], (tm, other)),
        send(3, bond_ext.at[both, last], bond_ext.at[both, low], (tm, other)),
        send(4, bond_ext.at[both, first], bond_ext.at[both, high], (tm, other)),
    ]
    next_guess = [
        send(0, ext.at[1, 0, own], ext.at[1, 2, own], (before, band)),
        send(5, ext.at[1, 0, last], ext.at[1, 2, low], (before, other)),
        send(6, ext.at[1, 0, first], ext.at[1, 2, high], (before, other)),
    ]

    def parity(size, axis):
        return lax.broadcasted_iota(jnp.int32, (size, lat), axis) % 2 == 0

    def rolled(value, by, axis):
        return pltpu.roll(value, by % value.shape[axis], axis)

    def make_tables(at, size, keep):
        row_even, col_even = parity(size, 0), parity(size, 1)
        horizontal, vertical = bond_ext[0, at : at + size, :], bond_ext[1, at : at + size, :]
        left, up = rolled(horizontal, 1, 1), rolled(vertical, 1, 0)
        strengths = (
            jnp.where(col_even, horizontal, left),
            jnp.where(col_even, left, horizontal),
            jnp.where(row_even, vertical, up),
            jnp.where(row_even, up, vertical),
        )
        begin, end = keep
        for q, s in enumerate(strengths):
            s = s[begin:end]
            tables[2 * q, at + begin : at + end, :] = jnp.where(s == 1, COSH, 1.0).astype(jnp.float32)
            tables[2 * q + 1, at + begin : at + end, :] = jnp.where(s == 1, SINH, 0.0).astype(jnp.float32)

    def pairs(value, colours, at):
        size = value.shape[0]
        row_even, col_even = parity(size, 0), parity(size, 1)
        for q in colours:
            axis, even = (1, col_even) if q < 2 else (0, row_even)
            plus, minus = rolled(value, -1, axis), rolled(value, 1, axis)
            partner = jnp.where(even, plus, minus) if q % 2 == 0 else jnp.where(even, minus, plus)
            value = tables[2 * q, at : at + size, :] * value + tables[2 * q + 1, at : at + size, :] * partner
        return value

    ahead = (0, 1, 2, 3)
    back = (3, 2, 1, 0)
    sign_before = jnp.where(tm == 0, -1.0, 1.0).astype(jnp.float32)
    sign_after = jnp.where(tm == n - 1, -1.0, 1.0).astype(jnp.float32)
    end = PAD + rows

    make_tables(PAD, rows, (0, rows))
    for s in (1, 0):
        expo[s, own, :] = jnp.exp(-coupling * ext[0, s, own, :])
        app[s, own, :] = pairs(expo[s, own, :] * ext[1, s, own, :], ahead, PAD)
        if s == 1:
            bulk = send(7, app.at[1, pl.ds(2 * PAD, rows - 2 * PAD)], app_in.at[pl.ds(PAD, rows - 2 * PAD)], (after, band))
    far_signals(far)
    for copy in edges:
        copy.wait_recv()
    make_tables(0, 2 * PAD, (0, 2 * PAD))
    make_tables(end - PAD, 2 * PAD, (PAD, 2 * PAD))
    tile = lax.broadcasted_iota(jnp.int32, (PAD, lat), 0)
    for s in (1, 0):
        for outer, block in ((0, 0), (end, end - PAD)):
            expo[s, outer : outer + PAD, :] = jnp.exp(-coupling * ext[0, s, outer : outer + PAD, :])
            here = slice(block, block + 2 * PAD)
            fixed = pairs(expo[s, here, :] * ext[1, s, here, :], ahead, block)
            if outer == 0:
                app[s, 0:PAD, :] = fixed[:PAD]
                mixed = jnp.where(tile == 0, fixed[PAD:], app[s, PAD : 2 * PAD, :])
                app[s, PAD : 2 * PAD, :] = mixed
            else:
                app[s, end : end + PAD, :] = fixed[PAD:]
                mixed = jnp.where(tile == PAD - 1, fixed[:PAD], app[s, end - PAD : end, :])
                app[s, end - PAD : end, :] = mixed
            if s == 1:
                edge_out[0 if outer == 0 else 1] = mixed
        if s == 1:
            edge_sent = send(8, edge_out, app_edge, (after, band))

    inner = slice(PAD, end)
    link = ext[1, 1] - app[0]
    pulled = pairs(link, back, 0)[inner]
    for copy in load_later[:2]:
        copy.wait()
    space = halves(sbasis[...])
    half = source[0] - ext[1, 0, own, :] + expo[0, own, :] * pulled
    link_own = link[inner]
    for copy in next_guess:
        copy.wait_recv()
    pulled = pairs(sign_after * ext[1, 2] - app[1], back, 0)[inner]
    residual = source[1] - (link_own - expo[1, own, :] * pulled)
    y[pl.ds(1, lat, 2), :] = dot(space, halves(residual), 1, 1)
    bulk.wait_recv()
    edge_sent.wait_recv()
    app_in[0:PAD, :] = app_edge[0]
    app_in[rows - PAD : rows, :] = app_edge[1]
    y[pl.ds(0, lat, 2), :] = dot(space, halves(half + sign_before * app_in[...]), 1, 1)

    pl.semaphore_wait(far, count - 1)
    def spread(k, src_of, dst):
        ss, rs = ssem.at[k], rsem.at[k]

        def put(t, b):
            pltpu.make_async_remote_copy(
                src_ref=src_of(t, b), dst_ref=dst, send_sem=ss, recv_sem=rs, device_id=(t, b), device_id_type=MESH
            ).start()

        pltpu.make_async_copy(src_of(tm, band), dst, rs).start()
        put(tm, other)

        def body(i, carry):
            t = wrap(tm + i, n)
            put(t, band)
            put(t, other)
            return carry

        lax.fori_loop(1, n, body, 0)

    spread(0, lambda t, b: y.at[pl.ds(4 * t + 2 * b, 2)], r.at[band, pl.ds(2 * tm, 2)])

    for copy in load_later[2:]:
        copy.wait()
    lam_c = lams[pl.ds(me, 1), :]
    chunk = 32

    def evaluate(i, carry):
        at = pl.ds(pl.multiple_of(i * chunk, chunk), chunk)
        lam_r = lams[at, :]
        shift = jnp.concatenate([lam_r + lam_c] * 2, axis=1)
        mu = weights[0:1, :] - shift
        direction = jnp.broadcast_to(weights[1:2, :], mu.shape)
        remaining = jnp.ones_like(mu)
        accum = jnp.zeros_like(mu)
        for step in range(ORDER):
            accum = accum + direction
            if step < ORDER - 1:
                remaining = remaining - mu * direction
                direction = weights[2 + 2 * step : 3 + 2 * step, :] * direction + weights[3 + 2 * step : 4 + 2 * step, :] * remaining
        poly[at, :] = relaxation * accum
        return carry

    lax.fori_loop(0, lat // chunk, evaluate, 0)
    slots = halves(tbasis[...])
    pltpu.make_async_copy(r, r, rsem.at[0]).wait()
    phonons = [
        send(9, ext.at[0, 1, own], phonon_prev, (after, band)),
        send(10, ext.at[0, 0, own], ext.at[0, 2, own], (before, band)),
    ]
    spectrum = dot(space, halves(jnp.concatenate([r[0], r[1]], axis=1)), 1, 1)
    spectrum = dot(halves(spectrum), slots, 1, 1) * poly[...]
    timed = dot(halves(spectrum), slots, 1, 0)
    timed = dot(halves(timed), space, 0, 0)
    v[0] = timed[:, :rows]
    v[1] = timed[:, rows:]
    spread(1, lambda t, b: v.at[b, pl.ds(2 * t, 2)], w.at[pl.ds(2 * me, 2)])
    for copy in phonons:
        copy.wait_recv()
    for s in range(2):
        here = ext[0, s, own, :]
        one_before = phonon_prev[...] if s == 0 else ext[0, 0, own, :]
        boson = stiffness * (2.0 * here - one_before - ext[0, s + 1, own, :]) + mass_term * here
        momentum[s] = momentum[s] - step_size * boson
    pltpu.make_async_copy(w, w, rsem.at[1]).wait()
    next_sol = []
    for s in range(2):
        sol[s, own, :] = ext[1, s, own, :] + dot(halves(w[pl.ds(s, lat, 2), :]), space, 0, 0)
        if s == 0:
            next_sol.append(send(11, sol.at[0, own], sol.at[2, own], (before, band)))
            next_sol.append(send(12, sol.at[0, last], sol.at[2, low], (before, other)))
            next_sol.append(send(13, sol.at[0, first], sol.at[2, high], (before, other)))
    sol_edges = [
        send(14, sol.at[both, last], sol.at[both, low], (tm, other)),
        send(15, sol.at[both, first], sol.at[both, high], (tm, other)),
    ]
    written = [load(0, sol.at[both, own], sol_out)]
    for copy in sol_edges:
        copy.wait_recv()
    applied = [pairs(expo[s] * sol[s], ahead, 0) for s in range(2)]
    for s in range(2):
        if s == 1:
            for copy in next_sol:
                copy.wait_recv()
        image = (sol[1] if s == 0 else sign_after * sol[2]) - applied[s]
        pulled = pairs(image, back, 0)[inner]
        fermion = (-2.0 * coupling) * expo[s, own, :] * sol[s, own, :] * pulled
        new[s] = momentum[s] - step_size * fermion
        written.append(load(1 + s, new.at[s], mom_out.at[s]))

    for copy in started:
        copy.wait_send()
    for k in range(2):
        sent = w.at[pl.ds(0, 2 * (2 * n - 1))]
        pltpu.make_async_copy(sent, sent, ssem.at[k]).wait()
    for copy in written:
        copy.wait()


def finish(sol_in, mom_in, sol_out, mom_out, held, sems):
    pieces = []
    for i, (src, dst) in enumerate(((sol_in, sol_out), (mom_in, mom_out))):
        for s in range(2):
            j = 2 * i + s
            pieces.append(
                (
                    pltpu.make_async_copy(src.at[s], held.at[j], sems.at[0, j]),
                    pltpu.make_async_copy(held.at[j], dst.at[s], sems.at[1, j]),
                )
            )
    for fetch, _ in pieces:
        fetch.start()
    for fetch, store in pieces:
        fetch.wait()
        store.start()
    for _, store in pieces:
        store.wait()


def shards(n, phonon, momentum, source, guess, bonds):
    slices, rows, lat = phonon.shape
    sbasis, lam = space_basis(lat)
    tbasis = time_basis(slices * n)
    weights = cheb_tables(slices * n)
    lams = np.ascontiguousarray(np.broadcast_to(lam.astype(np.float32)[:, None], (lat, 128)))
    hbm = pl.BlockSpec(memory_space=pltpu.HBM)
    total = rows + 2 * PAD
    f32 = jnp.float32
    made = pl.pallas_call(
        functools.partial(kernel, n),
        out_shape=[jax.ShapeDtypeStruct(phonon.shape, f32)] * 2,
        in_specs=[hbm] * 9,
        out_specs=[hbm] * 2,
        scratch_shapes=[
            pltpu.VMEM(phonon.shape, f32),
            pltpu.VMEM(phonon.shape, f32),
            pltpu.VMEM(tbasis.shape, f32),
            pltpu.VMEM(sbasis.shape, f32),
            pltpu.VMEM(weights.shape, f32),
            pltpu.VMEM(lams.shape, f32),
            pltpu.VMEM((2, 3, total, lat), f32),
            pltpu.VMEM((2, total, lat), jnp.int32),
            pltpu.VMEM((8, total, lat), f32),
            pltpu.VMEM((2, total, lat), f32),
            pltpu.VMEM((2, total, lat), f32),
            pltpu.VMEM((rows, lat), f32),
            pltpu.VMEM((2, PAD, lat), f32),
            pltpu.VMEM((2, PAD, lat), f32),
            pltpu.VMEM((rows, lat), f32),
            pltpu.VMEM((lat, lat), f32),
            pltpu.VMEM((2 * lat, rows), f32),
            pltpu.VMEM((2, slices * n, rows), f32),
            pltpu.VMEM((2, slices * n, rows), f32),
            pltpu.VMEM((2 * lat, rows), f32),
            pltpu.VMEM((3, total, lat), f32),
            pltpu.VMEM(phonon.shape, f32),
            pltpu.SemaphoreType.DMA((2,)),
            pltpu.SemaphoreType.DMA((2,)),
            pltpu.SemaphoreType.DMA((16,)),
            pltpu.SemaphoreType.DMA((16,)),
            pltpu.SemaphoreType.DMA((9,)),
            pltpu.SemaphoreType.REGULAR,
        ],
        compiler_params=pltpu.CompilerParams(
            collective_id=0, has_side_effects=True, vmem_limit_bytes=63 * 1024 * 1024
        ),
        cost_estimate=pl.CostEstimate(flops=400000000, bytes_accessed=3000000, transcendentals=200000),
    )(phonon, momentum, source, guess, bonds, jnp.asarray(tbasis), jnp.asarray(sbasis), jnp.asarray(weights), jnp.asarray(lams))
    return pl.pallas_call(
        finish,
        out_shape=[jax.ShapeDtypeStruct(phonon.shape, f32)] * 2,
        in_specs=[hbm] * 2,
        out_specs=[hbm] * 2,
        scratch_shapes=[pltpu.VMEM((4, rows, lat), f32), pltpu.SemaphoreType.DMA((2, 4))],
        compiler_params=pltpu.CompilerParams(vmem_limit_bytes=63 * 1024 * 1024),
        cost_estimate=pl.CostEstimate(flops=0, bytes_accessed=1048576, transcendentals=0),
    )(*made)


def solution(mesh):
    spec = P("tm", "band")
    return jax.shard_map(
        functools.partial(shards, mesh.shape["tm"]),
        mesh=mesh,
        in_specs=(spec, spec, spec, spec, P(None, "band", None)),
        out_specs=(spec, spec),
        check_vma=False,
    )
```

time: 54.8 us -> 48.6 us (0.89)
  Pallas kernels: 51.6 us -> 47.8 us
  local copies, waits for them, and re-layouts: 2.42 us -> 0 us
    pallas_call x1, Pallas kernels: 51.6 us -> 46 us  [shards(): pl.pallas_call(functools.partial(kernel, n), out_shape=[jax.ShapeDtypeStr...]
    unnamed x4 -> x0, local copies, waits for them, and re-layouts: 2.42 us -> none
    pallas_call x0 -> x1, Pallas kernels: none -> 1.82 us  [shards(): pl.pallas_call(finish, out_shape=[jax.ShapeDtypeStruct(phonon.shape, f32)...]
where the time goes in v3:
time: 48.6 us; the launch traced here: 48.4 us
  Pallas kernels  47.8 us (98%)
  between operations  0.64 us (1%)
    pallas_call x1, Pallas kernels, shards(): pl.pallas_call(functools.partial(kernel, n), out_shape=[jax.ShapeDtypeStr...  46 us
    pallas_call x1, Pallas kernels, shards(): pl.pallas_call(finish, out_shape=[jax.ShapeDtypeStruct(phonon.shape, f32)...  1.82 us

profile of v3, /device:TPU:1, one launch (start us, length us, event | category | flops | bytes accessed | tf_op | source)
XLA Modules:
  0.0 48.4 jit_solution(11522348538900129400)
XLA Ops:
  0.6 46.0 %shard_map.104 = (f32[2,128,256]{2,1,0:T(8,128)}, f32[2,128,256]{2,1,0:T(8,128)}) custom-call(f32[2,128,256]{2,1,0:T(8,128)} %phonon_in.1, f32[2,128,256]{2,1,0:T(8,128)} %momentum_in.1, f32[2,128,256]{2,1,0:T(8,128)} %source_in.1, f32[2,128,256]{2,1,0:T(8,128)} %guess_in.1, s32[2,128,256]{2,1,0:T(8,128)} %bonds_in.1, f32[256,256]{1,0:T(8,128)} %constant.8.clone.tbasis_in, ...), custom_call_target="tpu_custom_call" | custom-call | flops 400000000 | bytes 3000000 | tf_op jit(solution)/shard_map/pallas_call | solution.py:377
  46.6 1.8 %shard_map.105 = (f32[2,128,256]{2,1,0:T(8,128)}, f32[2,128,256]{2,1,0:T(8,128)}) custom-call(f32[2,128,256]{2,1,0:T(8,128)} %get-tuple-element.4.sol_in, f32[2,128,256]{2,1,0:T(8,128)} %get-tuple-element.5.mom_in), custom_call_target="tpu_custom_call" | custom-call | bytes 1048576 | tf_op jit(solution)/shard_map/pallas_call | solution.py:417

commit v4 on v3

--- a/solution.py
+++ b/solution.py
@@ -77,9 +77,9 @@
 
 
 def kernel(
-    n, phonon_in, momentum_in, source_in, guess_in, bonds_in, tbasis_in, sbasis_in, weights_in, lams_in, sol_out, mom_out,
-    source, momentum, tbasis, sbasis, weights, lams,
-    ext, bond_ext, tables, expo, app, app_in, app_edge, edge_out, phonon_prev, poly, y, r, v, w, sol, new,
+    n, phonon_in, momentum_in, source_in, guess_in, bonds_in, consts_in, sol_out, mom_out,
+    source, momentum, consts,
+    ext, bond_ext, tables, expo, app, app_in, app_edge, edge_out, phonon_prev, poly, y, r, v, w, sol,
     ssem, rsem, hs, hr, loads, far,
 ):
     rows, lat = source.shape[1:]
@@ -89,6 +89,8 @@
     me = 2 * tm + band
     after = wrap(tm + 1, n)
     before = jnp.where(tm == 0, n - 1, tm - 1)
+    tbasis, sbasis = consts.at[0:lat], consts.at[lat : 2 * lat]
+    lams, weights = consts.at[2 * lat : 3 * lat], consts.at[3 * lat : 3 * lat + 48]
     own = pl.ds(PAD, rows)
     both = pl.ds(0, 2)
 
@@ -126,11 +128,8 @@
     far_signals(barrier)
     load_later = [
         load(3, source_in, source),
-        load(4, sbasis_in, sbasis),
-        load(5, tbasis_in, tbasis),
-        load(6, weights_in, weights),
-        load(7, lams_in, lams),
-        load(8, momentum_in, momentum),
+        load(4, consts_in, consts),
+        load(5, momentum_in, momentum),
     ]
     for copy in load_first:
         copy.wait()
@@ -276,8 +275,7 @@
     def evaluate(i, carry):
         at = pl.ds(pl.multiple_of(i * chunk, chunk), chunk)
         lam_r = lams[at, :]
-        shift = jnp.concatenate([lam_r + lam_c] * 2, axis=1)
-        mu = weights[0:1, :] - shift
+        mu = weights[0:1, :] - (lam_r + lam_c)
         direction = jnp.broadcast_to(weights[1:2, :], mu.shape)
         remaining = jnp.ones_like(mu)
         accum = jnp.zeros_like(mu)
@@ -313,7 +311,9 @@
     pltpu.make_async_copy(w, w, rsem.at[1]).wait()
     next_sol = []
     for s in range(2):
-        sol[s, own, :] = ext[1, s, own, :] + dot(halves(w[pl.ds(s, lat, 2), :]), space, 0, 0)
+        value = ext[1, s, own, :] + dot(halves(w[pl.ds(s, lat, 2), :]), space, 0, 0)
+        sol[s, own, :] = value
+        sol_out[s] = value
         if s == 0:
             next_sol.append(send(11, sol.at[0, own], sol.at[2, own], (before, band)))
             next_sol.append(send(12, sol.at[0, last], sol.at[2, low], (before, other)))
@@ -322,7 +322,6 @@
         send(14, sol.at[both, last], sol.at[both, low], (tm, other)),
         send(15, sol.at[both, first], sol.at[both, high], (tm, other)),
     ]
-    written = [load(0, sol.at[both, own], sol_out)]
     for copy in sol_edges:
         copy.wait_recv()
     applied = [pairs(expo[s] * sol[s], ahead, 0) for s in range(2)]
@@ -333,36 +332,25 @@
         image = (sol[1] if s == 0 else sign_after * sol[2]) - applied[s]
         pulled = pairs(image, back, 0)[inner]
         fermion = (-2.0 * coupling) * expo[s, own, :] * sol[s, own, :] * pulled
-        new[s] = momentum[s] - step_size * fermion
-        written.append(load(1 + s, new.at[s], mom_out.at[s]))
+        mom_out[s] = momentum[s] - step_size * fermion
 
     for copy in started:
         copy.wait_send()
     for k in range(2):
         sent = w.at[pl.ds(0, 2 * (2 * n - 1))]
         pltpu.make_async_copy(sent, sent, ssem.at[k]).wait()
-    for copy in written:
+
+
+def finish(sol_in, mom_in, sol_out, mom_out, sems):
+    copies = [
+        pltpu.make_async_copy(src.at[s], dst.at[s], sems.at[i, s])
+        for i, (src, dst) in enumerate(((sol_in, sol_out), (mom_in, mom_out)))
+        for s in range(2)
+    ]
+    for copy in copies:
+        copy.start()
+    for copy in copies:
         copy.wait()
-
-
-def finish(sol_in, mom_in, sol_out, mom_out, held, sems):
-    pieces = []
-    for i, (src, dst) in enumerate(((sol_in, sol_out), (mom_in, mom_out))):
-        for s in range(2):
-            j = 2 * i + s
-            pieces.append(
-                (
-                    pltpu.make_async_copy(src.at[s], held.at[j], sems.at[0, j]),
-                    pltpu.make_async_copy(held.at[j], dst.at[s], sems.at[1, j]),
-                )
-            )
-    for fetch, _ in pieces:
-        fetch.start()
-    for fetch, store in pieces:
-        fetch.wait()
-        store.start()
-    for _, store in pieces:
-        store.wait()
 
 
 def shards(n, phonon, momentum, source, guess, bonds):
@@ -370,22 +358,21 @@
     sbasis, lam = space_basis(lat)
     tbasis = time_basis(slices * n)
     weights = cheb_tables(slices * n)
-    lams = np.ascontiguousarray(np.broadcast_to(lam.astype(np.float32)[:, None], (lat, 128)))
+    lams = np.broadcast_to(lam.astype(np.float32)[:, None], (lat, lat))
+    consts = np.concatenate([tbasis, sbasis, lams, weights])
+    vmem = pl.BlockSpec(memory_space=pltpu.VMEM)
     hbm = pl.BlockSpec(memory_space=pltpu.HBM)
     total = rows + 2 * PAD
     f32 = jnp.float32
     made = pl.pallas_call(
         functools.partial(kernel, n),
         out_shape=[jax.ShapeDtypeStruct(phonon.shape, f32)] * 2,
-        in_specs=[hbm] * 9,
-        out_specs=[hbm] * 2,
+        in_specs=[hbm] * 6,
+        out_specs=[vmem] * 2,
         scratch_shapes=[
             pltpu.VMEM(phonon.shape, f32),
             pltpu.VMEM(phonon.shape, f32),
-            pltpu.VMEM(tbasis.shape, f32),
-            pltpu.VMEM(sbasis.shape, f32),
-            pltpu.VMEM(weights.shape, f32),
-            pltpu.VMEM(lams.shape, f32),
+            pltpu.VMEM(consts.shape, f32),
             pltpu.VMEM((2, 3, total, lat), f32),
             pltpu.VMEM((2, total, lat), jnp.int32),
             pltpu.VMEM((8, total, lat), f32),
@@ -401,26 +388,25 @@
             pltpu.VMEM((2, slices * n, rows), f32),
             pltpu.VMEM((2 * lat, rows), f32),
             pltpu.VMEM((3, total, lat), f32),
-            pltpu.VMEM(phonon.shape, f32),
             pltpu.SemaphoreType.DMA((2,)),
             pltpu.SemaphoreType.DMA((2,)),
             pltpu.SemaphoreType.DMA((16,)),
             pltpu.SemaphoreType.DMA((16,)),
-            pltpu.SemaphoreType.DMA((9,)),
+            pltpu.SemaphoreType.DMA((6,)),
             pltpu.SemaphoreType.REGULAR,
         ],
         compiler_params=pltpu.CompilerParams(
-            collective_id=0, has_side_effects=True, vmem_limit_bytes=63 * 1024 * 1024
+            collective_id=0, has_side_effects=True, vmem_limit_bytes=(53 * 1024 + 256) * 1024
         ),
         cost_estimate=pl.CostEstimate(flops=400000000, bytes_accessed=3000000, transcendentals=200000),
-    )(phonon, momentum, source, guess, bonds, jnp.asarray(tbasis), jnp.asarray(sbasis), jnp.asarray(weights), jnp.asarray(lams))
+    )(phonon, momentum, source, guess, bonds, jnp.asarray(consts))
     return pl.pallas_call(
         finish,
         out_shape=[jax.ShapeDtypeStruct(phonon.shape, f32)] * 2,
-        in_specs=[hbm] * 2,
+        in_specs=[vmem] * 2,
         out_specs=[hbm] * 2,
-        scratch_shapes=[pltpu.VMEM((4, rows, lat), f32), pltpu.SemaphoreType.DMA((2, 4))],
-        compiler_params=pltpu.CompilerParams(vmem_limit_bytes=63 * 1024 * 1024),
+        scratch_shapes=[pltpu.SemaphoreType.DMA((2, 2))],
+        compiler_params=pltpu.CompilerParams(vmem_limit_bytes=8 * 1024 * 1024),
         cost_estimate=pl.CostEstimate(flops=0, bytes_accessed=1048576, transcendentals=0),
     )(*made)
 

time: 48.6 us -> 46.9 us (0.965)
  Pallas kernels: 47.8 us -> 46.2 us
    pallas_call x1, Pallas kernels: 1.82 us -> 0.82 us  [shards(): pl.pallas_call(finish, out_shape=[jax.ShapeDtypeStruct(phonon.shape, f32)...]
    pallas_call x1, Pallas kernels: 46 us -> 45.4 us  [shards(): pl.pallas_call(functools.partial(kernel, n), out_shape=[jax.ShapeDtypeStr...]
where the time goes in v4:
time: 46.9 us; the launch traced here: 46.8 us
  Pallas kernels  46.2 us (99%)
  between operations  0.64 us (1%)
    pallas_call x1, Pallas kernels, shards(): pl.pallas_call(functools.partial(kernel, n), out_shape=[jax.ShapeDtypeStr...  45.4 us

profile of v4, /device:TPU:1, one launch (start us, length us, event | category | flops | bytes accessed | tf_op | source)
XLA Modules:
  0.0 46.8 jit_solution(4216591462210748907)
XLA Ops:
  0.6 45.4 %shard_map.77 = (f32[2,128,256]{2,1,0:T(8,128)S(1)}, f32[2,128,256]{2,1,0:T(8,128)S(1)}) custom-call(f32[2,128,256]{2,1,0:T(8,128)} %phonon_in.1, f32[2,128,256]{2,1,0:T(8,128)} %momentum_in.1, f32[2,128,256]{2,1,0:T(8,128)} %source_in.1, f32[2,128,256]{2,1,0:T(8,128)} %guess_in.1, s32[2,128,256]{2,1,0:T(8,128)} %bonds_in.1, f32[816,256]{1,0:T(8,128)} %constant.2.clone.consts_in), custom_call_target="tpu_custom_call" | custom-call | flops 400000000 | bytes 3000000 | tf_op jit(solution)/shard_map/pallas_call | solution.py:367
  46.0 0.8 %shard_map.78 = (f32[2,128,256]{2,1,0:T(8,128)}, f32[2,128,256]{2,1,0:T(8,128)}) custom-call(f32[2,128,256]{2,1,0:T(8,128)S(1)} %get-tuple-element.4.sol_in, f32[2,128,256]{2,1,0:T(8,128)S(1)} %get-tuple-element.5.mom_in), custom_call_target="tpu_custom_call" | custom-call | bytes 1048576 | tf_op jit(solution)/shard_map/pallas_call | solution.py:403

commit v5 on v4

--- a/solution.py
+++ b/solution.py
@@ -263,7 +263,7 @@
             put(t, other)
             return carry
 
-        lax.fori_loop(1, n, body, 0)
+        lax.fori_loop(1, n, body, 0, unroll=4)
 
     spread(0, lambda t, b: y.at[pl.ds(4 * t + 2 * b, 2)], r.at[band, pl.ds(2 * tm, 2)])
 

time: 46.9 us -> 46.7 us (level)
  no operation moved by 1% of the time
where the time goes in v5:
time: 46.7 us; the launch traced here: 46.6 us
  Pallas kernels  45.9 us (98%)
  between operations  0.64 us (1%)
    pallas_call x1, Pallas kernels, shards(): pl.pallas_call(functools.partial(kernel, n), out_shape=[jax.ShapeDtypeStr...  45.1 us

profile of v5, /device:TPU:1, one launch (start us, length us, event | category | flops | bytes accessed | tf_op | source)
XLA Modules:
  0.0 46.6 jit_solution(1499317679871565516)
XLA Ops:
  0.6 45.1 %shard_map.77 = (f32[2,128,256]{2,1,0:T(8,128)S(1)}, f32[2,128,256]{2,1,0:T(8,128)S(1)}) custom-call(f32[2,128,256]{2,1,0:T(8,128)} %phonon_in.1, f32[2,128,256]{2,1,0:T(8,128)} %momentum_in.1, f32[2,128,256]{2,1,0:T(8,128)} %source_in.1, f32[2,128,256]{2,1,0:T(8,128)} %guess_in.1, s32[2,128,256]{2,1,0:T(8,128)} %bonds_in.1, f32[816,256]{1,0:T(8,128)} %constant.2.clone.consts_in), custom_call_target="tpu_custom_call" | custom-call | flops 400000000 | bytes 3000000 | tf_op jit(solution)/shard_map/pallas_call | solution.py:367
  45.7 0.8 %shard_map.78 = (f32[2,128,256]{2,1,0:T(8,128)}, f32[2,128,256]{2,1,0:T(8,128)}) custom-call(f32[2,128,256]{2,1,0:T(8,128)S(1)} %get-tuple-element.4.sol_in, f32[2,128,256]{2,1,0:T(8,128)S(1)} %get-tuple-element.5.mom_in), custom_call_target="tpu_custom_call" | custom-call | bytes 1048576 | tf_op jit(solution)/shard_map/pallas_call | solution.py:403

commit v6 on v5

--- a/solution.py
+++ b/solution.py
@@ -239,33 +239,37 @@
     pulled = pairs(sign_after * ext[1, 2] - app[1], back, 0)[inner]
     residual = source[1] - (link_own - expo[1, own, :] * pulled)
     y[pl.ds(1, lat, 2), :] = dot(space, halves(residual), 1, 1)
+    def spread(k, src_of, dst):
+        ss, rs = ssem.at[k], rsem.at[k]
+
+        def put(t, b):
+            pltpu.make_async_remote_copy(
+                src_ref=src_of(t, b), dst_ref=dst, send_sem=ss, recv_sem=rs, device_id=(t, b), device_id_type=MESH
+            ).start()
+
+        pltpu.make_async_copy(src_of(tm, band), dst, rs).start()
+        put(tm, other)
+
+        def body(i, carry):
+            t = wrap(tm + i, n)
+            put(t, band)
+            put(t, other)
+            return carry
+
+        lax.fori_loop(1, n, body, 0, unroll=4)
+
+    def part_out(s):
+        spread(0, lambda t, b: y.at[pl.ds(4 * t + 2 * b + s, 1)], r.at[band, pl.ds(2 * tm + s, 1)])
+
+    pl.semaphore_wait(far, count - 1)
+    part_out(1)
     bulk.wait_recv()
     edge_sent.wait_recv()
     app_in[0:PAD, :] = app_edge[0]
     app_in[rows - PAD : rows, :] = app_edge[1]
     y[pl.ds(0, lat, 2), :] = dot(space, halves(half + sign_before * app_in[...]), 1, 1)
 
-    pl.semaphore_wait(far, count - 1)
-    def spread(k, src_of, dst):
-        ss, rs = ssem.at[k], rsem.at[k]
-
-        def put(t, b):
-            pltpu.make_async_remote_copy(
-                src_ref=src_of(t, b), dst_ref=dst, send_sem=ss, recv_sem=rs, device_id=(t, b), device_id_type=MESH
-            ).start()
-
-        pltpu.make_async_copy(src_of(tm, band), dst, rs).start()
-        put(tm, other)
-
-        def body(i, carry):
-            t = wrap(tm + i, n)
-            put(t, band)
-            put(t, other)
-            return carry
-
-        lax.fori_loop(1, n, body, 0, unroll=4)
-
-    spread(0, lambda t, b: y.at[pl.ds(4 * t + 2 * b, 2)], r.at[band, pl.ds(2 * tm, 2)])
+    part_out(0)
 
     for copy in load_later[2:]:
         copy.wait()

time: 46.7 us -> 46.3 us (level)
  Pallas kernels: 45.9 us -> 45.2 us
    pallas_call x1, Pallas kernels: 45.1 us -> 44.4 us  [shards(): pl.pallas_call(functools.partial(kernel, n), out_shape=[jax.ShapeDtypeStr...]
where the time goes in v6:
time: 46.3 us; the launch traced here: 45.8 us
  Pallas kernels  45.2 us (98%)
  between operations  0.64 us (1%)
    pallas_call x1, Pallas kernels, shards(): pl.pallas_call(functools.partial(kernel, n), out_shape=[jax.ShapeDtypeStr...  44.4 us

profile of v6, /device:TPU:1, one launch (start us, length us, event | category | flops | bytes accessed | tf_op | source)
XLA Modules:
  0.0 45.8 jit_solution(18108152645075570574)
XLA Ops:
  0.6 44.4 %shard_map.77 = (f32[2,128,256]{2,1,0:T(8,128)S(1)}, f32[2,128,256]{2,1,0:T(8,128)S(1)}) custom-call(f32[2,128,256]{2,1,0:T(8,128)} %phonon_in.1, f32[2,128,256]{2,1,0:T(8,128)} %momentum_in.1, f32[2,128,256]{2,1,0:T(8,128)} %source_in.1, f32[2,128,256]{2,1,0:T(8,128)} %guess_in.1, s32[2,128,256]{2,1,0:T(8,128)} %bonds_in.1, f32[816,256]{1,0:T(8,128)} %constant.2.clone.consts_in), custom_call_target="tpu_custom_call" | custom-call | flops 400000000 | bytes 3000000 | tf_op jit(solution)/shard_map/pallas_call | solution.py:371
  45.0 0.8 %shard_map.78 = (f32[2,128,256]{2,1,0:T(8,128)}, f32[2,128,256]{2,1,0:T(8,128)}) custom-call(f32[2,128,256]{2,1,0:T(8,128)S(1)} %get-tuple-element.4.sol_in, f32[2,128,256]{2,1,0:T(8,128)S(1)} %get-tuple-element.5.mom_in), custom_call_target="tpu_custom_call" | custom-call | bytes 1048576 | tf_op jit(solution)/shard_map/pallas_call | solution.py:407
